TPU v7x, 256 devices: a whole 4x4x8 slice. The times are simulated.
256 devices in a mesh: tm: 16 (over y, x), pair: 16 (over z, core).
Axes of the slice: x: 4, y: 4, z: 8, core: 2. Of those that a mesh axis runs over, the one named last changes fastest.
Arguments:
- record: bfloat16 [8192, 16, 256], P('tm', None, 'pair'), may hold values from -6 to 6
- partners: int32 [4096, 64], P(('tm', 'pair')), may hold values from 0 to 4095, as said below
- offsets: int32 [15], replicated, may hold values from 0 to 7168, as said below
Outputs:
- correlations: float32 [4096, 64, 512], P(('tm', 'pair'))
Inputs may be any that keep to these rules, and one draw needn't show every extreme that they name: `partners`: row k lists 64 different channels, none equal to k, all with the same value of channel // 256 as k, and each within 400 channels of k. offsets[0] is 0, offsets[14] is 7168, and offsets[s] lies within 128 of s * 512.
All inputs are finite; a program needn't handle non-finite values.
Results may differ from a plain program's by a relative error of at most 0.0051.
Values may be sent and summed in bfloat16 or wider, within the bound.
No kernel may reach another device: no remote copies, remote signals or barrier semaphores. Data moves between devices by JAX's collectives and lax.ppermute only.
A program may use at most 128 MiB of HBM per device.

v0:
```python
import functools
import math

import jax
import jax.numpy as jnp
import numpy as np
from jax import lax
from jax.experimental import pallas as pl
from jax.experimental.pallas import tpu as pltpu
from jax.sharding import PartitionSpec as P

SEG = 1024
NF = 512
NLAG = 512
SEGS = 15
SLOTS = 16
NPART = 64
TSAMP = 8192
SHARDS = 16
SHARD = TSAMP // SHARDS
SECT = 256
OWN = 16
FB = 8
BLOCKS = NF // FB
F32 = jnp.float32
BF16 = jnp.bfloat16
NT = (((1,), (1,)), ((), ()))
NN = (((1,), (0,)), ((), ()))


def build_tables():
    column = np.arange(2 * NF)
    imag_part = column >= NF
    frequency = column % NF
    samples = np.arange(SEG)
    phase = (samples[:, None] * frequency[None, :] % SEG).astype(np.float32) * np.float32(2.0 * math.pi / SEG)
    taper = 0.5 - 0.5 * np.cos(samples.astype(np.float32) * np.float32(2.0 * math.pi / SEG))
    forward = taper[:, None] * np.where(imag_part[None, :], -np.sin(phase), np.cos(phase))
    lag = np.arange(NLAG) - NLAG // 2
    lag_phase = (frequency[:, None] * lag[None, :] % SEG).astype(np.float32) * np.float32(2.0 * math.pi / SEG)
    inverse = np.where(imag_part[:, None], -np.sin(lag_phase), np.cos(lag_phase))
    return np.ascontiguousarray(forward.T.astype(jnp.bfloat16)), inverse.astype(jnp.bfloat16)


def dot(a, b, dims):
    return lax.dot_general(a, b, dims, preferred_element_type=F32)


def kernel(offsets, series_hbm, forward, inverse, spread, picks, out_hbm,
           series, piece, spectrum, white, grams, chosen, result, in_sem, out_sem):
    copies = [
        pltpu.make_async_copy(series_hbm.at[:, t], series.at[:, :, pl.ds(t * SHARD, SHARD)], in_sem.at[t])
        for t in range(SHARDS)
    ]
    for c in copies:
        c.start()
    white[:, :, SEGS] = jnp.zeros((BLOCKS, 2, FB, SECT), F32)
    lane = lax.broadcasted_iota(jnp.int32, (SECT, 128), 1)
    for c in copies:
        c.wait()

    def segment(s, carry):
        start = offsets[s]
        base = start // 128
        off = start % 128
        back = (128 - off) % 128
        keep = lane < 128 - off

        def tile(i):
            at = pl.multiple_of(jnp.minimum(base + i, TSAMP // 128 - 1) * 128, 128)
            rows = series[:, :, pl.ds(at, 128)].reshape(SECT, 128)
            return pltpu.roll(rows.astype(F32), back, 1)

        here = tile(0)
        for i in range(SEG // 128):
            after = tile(i + 1)
            piece[:, i * 128:(i + 1) * 128] = jnp.where(keep, here, after).astype(BF16)
            here = after
        spectrum[...] = dot(forward[...], piece[...], NT)
        total = jnp.zeros((FB, SECT), F32)
        for b in range(BLOCKS):
            re = spectrum[b * FB:(b + 1) * FB, :]
            im = spectrum[NF + b * FB:NF + (b + 1) * FB, :]
            total += re * re + im * im
        water = jnp.sum(total, axis=0, keepdims=True) * (1.0 / NF) + 1e-06
        for b in range(BLOCKS):
            re = spectrum[b * FB:(b + 1) * FB, :]
            im = spectrum[NF + b * FB:NF + (b + 1) * FB, :]
            factor = lax.rsqrt(re * re + im * im + water)
            white[b, 0, s] = re * factor
            white[b, 1, s] = im * factor
        return carry

    lax.fori_loop(0, SEGS, segment, 0)

    half = SLOTS * FB
    mask = (
        lax.broadcasted_iota(jnp.int32, (OWN * FB, 2 * half), 0) % FB
        == lax.broadcasted_iota(jnp.int32, (OWN * FB, 2 * half), 1) % FB
    )
    zero = jnp.zeros((OWN * FB, 2 * half), F32)

    def gram(b):
        rows = white[b].reshape(2 * half, SECT).astype(BF16)
        own = dot(spread[...], rows, NT)
        own = jnp.where(mask, own, zero)
        turned = jnp.concatenate([-own[:, half:], own[:, :half]], axis=1)
        both = jnp.concatenate([own, turned], axis=0).astype(BF16)
        return dot(both, rows, NN).reshape(2, OWN, FB, SECT)

    def pair_of_blocks(b, carry):
        low, high = gram(2 * b), gram(2 * b + 1)
        for k in range(OWN):
            for ri in range(2):
                grams[k, ri, b] = jnp.concatenate([low[ri, k], high[ri, k]], axis=0).astype(BF16)
        return carry

    lax.fori_loop(0, BLOCKS // 2, pair_of_blocks, 0)

    GROUP = 4
    outs = [
        pltpu.make_async_copy(
            result.at[pl.ds(g * GROUP, GROUP)], out_hbm.at[pl.ds(g * GROUP, GROUP)], out_sem.at[g]
        )
        for g in range(OWN // GROUP)
    ]
    for g in range(OWN // GROUP):
        for k in range(g * GROUP, (g + 1) * GROUP):
            crossed = dot(picks[k], grams[k].reshape(2 * NF, SECT), NT)
            chosen[k % GROUP] = crossed.astype(BF16)
        lags = dot(chosen[...].reshape(GROUP * NPART, 2 * NF), inverse[...], NN) * (1.0 / math.sqrt(NF))
        result[g * GROUP:(g + 1) * GROUP] = lags.reshape(GROUP, NPART, NLAG)
        outs[g].start()
    for o in outs:
        o.wait()


def per_device(record, partners, offsets):
    forward, inverse = (jnp.asarray(t) for t in build_tables())
    by_section = jnp.transpose(record, (1, 2, 0))
    mine = lax.all_to_all(by_section, "tm", split_axis=0, concat_axis=0, tiled=True)
    series = lax.all_gather(mine, "pair", axis=0)
    place = lax.axis_index("pair")
    channel = lax.broadcasted_iota(jnp.int32, (OWN * FB, SECT), 1)
    own = place * OWN + lax.broadcasted_iota(jnp.int32, (OWN * FB, SECT), 0) // FB
    spread = (channel == own).astype(BF16)
    picks = ((partners % SECT)[:, :, None] == jnp.arange(SECT, dtype=jnp.int32)).astype(BF16)
    vmem = pl.BlockSpec(memory_space=pltpu.VMEM)
    any_ = pl.BlockSpec(memory_space=pl.ANY)
    return pl.pallas_call(
        kernel,
        out_shape=jax.ShapeDtypeStruct((OWN, NPART, NLAG), F32),
        in_specs=[pl.BlockSpec(memory_space=pltpu.SMEM), any_, vmem, vmem, vmem, vmem],
        out_specs=any_,
        scratch_shapes=[
            pltpu.VMEM((SECT // OWN, OWN, TSAMP), BF16),
            pltpu.VMEM((SECT, SEG), BF16),
            pltpu.VMEM((2 * NF, SECT), F32),
            pltpu.VMEM((BLOCKS, 2, SLOTS, FB, SECT), F32),
            pltpu.VMEM((OWN, 2, BLOCKS // 2, 2 * FB, SECT), BF16),
            pltpu.VMEM((4, NPART, 2 * NF), BF16),
            pltpu.VMEM((OWN, NPART, NLAG), F32),
            pltpu.SemaphoreType.DMA((SHARDS,)),
            pltpu.SemaphoreType.DMA((OWN // 4,)),
        ],
        compiler_params=pltpu.CompilerParams(vmem_limit_bytes=56 * 1024 * 1024),
        name="correlate",
    )(offsets, series, forward, inverse, spread, picks)


def solution(mesh):
    in_specs = (P("tm", None, "pair"), P(("tm", "pair"), None), P())
    out_specs = P(("tm", "pair"), None, None)
    return jax.shard_map(
        per_device, mesh=mesh, in_specs=in_specs, out_specs=out_specs, check_vma=False
    )
```

profile of v0, /device:TPU:1, one launch (start us, length us, event | category | flops | bytes accessed | tf_op | source)
XLA Modules:
  0.0 114.9 jit_solution(1460625762518610066)
XLA Ops:
  6.5 0.0 all-gather.3.cloned.1.call-start
  6.5 15.2 %all_to_all.5 = bf16[16,16,512]{2,1,0:T(8,128)(2,1)} all-to-all(bf16[16,16,512]{2,1,0:T(8,128)(2,1)} %bitcast.3), channel_id=1, replica_groups=mesh['tm'=16,'pair'=16] {'tm'}, dimensions={0} | all-to-all | bytes 524288 | tf_op jit(solution)/shard_map/all_to_all | solution.py:141
  21.8 0.0 all-gather.3.cloned.1.call-update
  21.8 0.7 add_select_fusion
  22.5 0.7 fusion.1.spread
  23.3 1.0 fusion.picks
  24.3 40.7 %all-gather.3.cloned.1.call-done = bf16[256,16,512]{2,1,0:T(8,128)(2,1)} async-done(((bf16[16,16,512]{2,1,0:T(8,128)(2,1)}), bf16[256,16,512]{2,1,0:T(8,128)(2,1)}) %all-gather.3.cloned.1.call-update) | async-done | bytes 4194320 | tf_op jit(solution)/shard_map/all_gather | solution.py:142
  64.9 43.1 %correlate.1 = f32[16,64,512]{2,1,0:T(8,128)} custom-call(s32[15]{0:T(128)} %offsets.1, bf16[16,16,16,512]{3,2,1,0:T(8,128)(2,1)} %bitcast.2, bf16[1024,1024]{1,0:T(8,128)(2,1)} %constant.44.clone.forward, bf16[1024,512]{1,0:T(8,128)(2,1)} %constant.45.clone.inverse, bf16[128,256]{1,0:T(8,128)(2,1)} %fusion.1.spread, bf16[16,64,256]{2,1,0:T(8,128)(2,1)} %fusion.picks), custom_call_target="tpu_custom_call" | custom-call | tf_op jit(solution)/shard_map/correlate/pallas_call | solution.py:150
  (2 shorter events, 0.0 us)
Async XLA Ops:
  6.5 58.4 %all-gather.3.cloned.1.call-start = ((), (), s32[]{:S(2)}) async-start(), calls=%async_computation.1 | async-start | bytes 4456448 | tf_op jit(solution)/shard_map/all_gather | solution.py:142
Sparse Core Ops, SparseCore 0:
  21.9 42.9 all-gather.2
where the time goes:
time: 115 us
  Pallas kernels  43.1 us (37%)
  waiting for transfers between devices  40.7 us (35%)
  blocking collectives  15.2 us (13%)
  between operations  13.4 us (12%)
  other arithmetic  2.47 us (2%)
    pallas_call x1, Pallas kernels, per_device(): pl.pallas_call(kernel, out_shape=jax.ShapeDtypeStruct((OWN, NPART, NLAG),...  43.1 us
    all_gather x1, waiting for transfers between devices, per_device(): series = lax.all_gather(mine, 'pair', axis=0)  40.7 us
    all_to_all x1, blocking collectives, per_device(): lax.all_to_all(by_section, 'tm', split_axis=0, concat_axis=0, tiled=True)  15.2 us
  transfers between devices with their start and end apart: 1, of which 1 were waited for; matrix products, arithmetic and copies ran while one was open for 2% of the time, Pallas kernels for 0%

commit v1 on v0

v1 whole, which is shorter than its diff:
```python
import functools
import math

import jax
import jax.numpy as jnp
import numpy as np
from jax import lax
from jax.experimental import pallas as pl
from jax.experimental.pallas import tpu as pltpu
from jax.sharding import PartitionSpec as P

SEG = 1024
NF = 512
NLAG = 512
SEGS = 15
PAIRS = 8
NPART = 64
SHARDS = 16
SHARD = 512
SECT = 256
OWN = 16
HALF = 128
FB = 8
BLOCKS = NF // FB
TILES = 16
F32 = jnp.float32
BF16 = jnp.bfloat16
NT = (((1,), (1,)), ((), ()))
NN = (((1,), (0,)), ((), ()))


def slots():
    q = np.arange(128)
    freq = np.concatenate([q, 512 - q, 256 + q, 256 - q])
    freq[128], freq[384] = 128, 384
    sign = np.where(np.arange(512) < 384, 1.0, -1.0)
    return freq, sign


def build_tables():
    samples = np.arange(SEG)
    unit = np.float32(2.0 * math.pi / SEG)
    taper = (0.5 - 0.5 * np.cos(samples.astype(np.float32) * unit)).astype(np.float32)
    q = np.arange(128)
    phase = (q[:, None] * samples[None, :] % SEG).astype(np.float32) * unit
    cosine, sine = taper * np.cos(phase), -taper * np.sin(phase)
    eighth = (128 * samples % SEG).astype(np.float32) * unit
    sine[0] = np.where(samples % 4 == 2, -taper * np.sin(eighth), taper * np.cos(eighth))
    sine[0] = np.where(samples % 4 == 2, -1.0, np.where(samples % 4 == 3, -1.0, 1.0)) * sine[0]
    forward = np.concatenate([cosine, sine]).reshape(256, 256, 4).transpose(2, 0, 1)
    freq, sign = slots()
    lag = np.arange(NLAG) - NLAG // 2
    lag_phase = (freq[:, None] * lag[None, :] % SEG).astype(np.float32) * unit
    inverse = np.concatenate([np.cos(lag_phase), -sign[:, None] * np.sin(lag_phase)])
    return np.ascontiguousarray(forward).astype(jnp.bfloat16), inverse.astype(jnp.bfloat16)


def dot(a, b, dims):
    return lax.dot_general(a, b, dims, preferred_element_type=F32)


def cut_pieces(offsets, series, piece, u, slot):
    lane = lax.broadcasted_iota(jnp.int32, (HALF, 128), 1)
    for s2 in range(2):
        start = offsets[min(2 * u + s2, SEGS - 1)]
        for r in range(4):
            first = start + r
            group = pl.multiple_of((first & 3) * 128, 128)
            at = first >> 2
            tile, off = at >> 7, at & 127
            back = (128 - off) & 127
            keep = lane < 128 - off
            turned = []
            for i in range(3):
                t = jnp.minimum(tile + i, SHARDS - 1)
                rows = series[:, t, :, pl.ds(group, 128)].reshape(HALF, 128)
                turned.append(pltpu.roll(rows.astype(F32), back, 1))
            for i in range(2):
                piece[slot, r, s2 * HALF:(s2 + 1) * HALF, i * 128:(i + 1) * 128] = jnp.where(
                    keep, turned[i], turned[i + 1]
                ).astype(BF16)


def transform(forward, piece, part, slot):
    for r in range(4):
        part[slot, r] = dot(forward[r], piece[slot, r], NT)


def whiten(part, full, white, u, slot, lanes):
    head = lax.broadcasted_iota(jnp.int32, (FB, SECT), 0) == 0
    total = jnp.zeros((FB, SECT), F32)
    for i in range(TILES):
        c = [part[slot, r, i * FB:(i + 1) * FB, :] for r in range(4)]
        s = [part[slot, r, HALF + i * FB:HALF + (i + 1) * FB, :] for r in range(4)]
        a, b = c[0] + c[2], c[0] - c[2]
        e, g = s[0] + s[2], s[0] - s[2]
        d, k = c[1] - c[3], s[1] - s[3]
        p, h = c[1] + c[3], s[1] + s[3]
        re = [a + p, a - p, b + k, b - k]
        im = [e + h, h - e, g - d, g + d]
        if i == 0:
            im[0] = jnp.where(head, 0.0, im[0])
            re[1] = jnp.where(head, s[0] + k, re[1])
            im[1] = jnp.where(head, -h - s[2], im[1])
            re[2] = jnp.where(head, b, re[2])
            im[2] = jnp.where(head, -d, im[2])
            re[3] = jnp.where(head, s[0] - k, re[3])
            im[3] = jnp.where(head, h - s[2], im[3])
        for j in range(4):
            full[0, j, i], full[1, j, i] = re[j], im[j]
            total += re[j] * re[j] + im[j] * im[j]
    water = jnp.sum(total, axis=0, keepdims=True) * (1.0 / NF) + 1e-06
    for i in range(TILES):
        for j in range(4):
            re, im = full[0, j, i], full[1, j, i]
            factor = lax.rsqrt(re * re + im * im + water)
            for ri, v in ((0, re * factor), (1, im * factor)):
                white[j * TILES + i, ri, u, :, lanes] = jnp.concatenate(
                    [v[:, :HALF], v[:, HALF:]], axis=0
                ).astype(BF16)


def spectra(offsets, series, forward, piece, part, full, white, lanes):
    cut_pieces(offsets, series, piece, 0, 0)
    for u in range(PAIRS):
        transform(forward, piece, part, u % 2)
        if u + 1 < PAIRS:
            cut_pieces(offsets, series, piece, u + 1, (u + 1) % 2)
        whiten(part, full.at[u % 2], white, u, u % 2, lanes)


def near_kernel(offsets, *refs):
    blocks, (forward, white, series, piece, part, full, sem) = refs[:8], refs[8:]
    copies = [pltpu.make_async_copy(b, series.at[i], sem.at[i]) for i, b in enumerate(blocks)]
    for c in copies:
        c.start()
    for c in copies:
        c.wait()
    spectra(offsets, series, forward, piece, part, full, white, slice(0, HALF))


def own_kernel(white, spread, own):
    row = lax.broadcasted_iota(jnp.int32, (HALF, 2 * HALF), 0)
    column = lax.broadcasted_iota(jnp.int32, (HALF, 2 * HALF), 1)
    mask = (row % FB == column % FB) & (column % HALF < SEGS * FB)

    def rows(b, carry):
        spreaded = dot(spread[...], white[b].reshape(2 * HALF, HALF), NT)
        own[b] = jnp.where(mask, spreaded, 0.0).astype(BF16)
        return carry

    lax.fori_loop(0, BLOCKS, rows, 0, unroll=8)


def scratch():
    return [
        pltpu.VMEM((8, SHARDS, OWN, SHARD), BF16),
        pltpu.VMEM((2, 4, SECT, 256), BF16),
        pltpu.VMEM((2, 4, SECT, SECT), F32),
        pltpu.VMEM((2, 2, 4, TILES, FB, SECT), F32),
    ]


VMEM_SPEC = pl.BlockSpec(memory_space=pltpu.VMEM)
ANY_SPEC = pl.BlockSpec(memory_space=pl.ANY)
SMEM_SPEC = pl.BlockSpec(memory_space=pltpu.SMEM)


def near_spectra(offsets, blocks, forward):
    return pl.pallas_call(
        near_kernel,
        out_shape=jax.ShapeDtypeStruct((BLOCKS, 2, PAIRS, 2 * FB, HALF), BF16),
        in_specs=[SMEM_SPEC] + [ANY_SPEC] * 8 + [VMEM_SPEC],
        out_specs=VMEM_SPEC,
        scratch_shapes=scratch() + [pltpu.SemaphoreType.DMA((8,))],
        compiler_params=pltpu.CompilerParams(vmem_limit_bytes=16 * 1024 * 1024),
        cost_estimate=pl.CostEstimate(flops=5_000_000_000, bytes_accessed=7_000_000, transcendentals=0),
        name="near_spectra",
    )(offsets, *blocks, forward)


def own_operand(white):
    spread = (np.arange(HALF)[:, None] // FB == np.arange(HALF)[None, :]).astype(jnp.bfloat16)
    return pl.pallas_call(
        own_kernel,
        out_shape=jax.ShapeDtypeStruct((BLOCKS, HALF, SECT), BF16),
        in_specs=[VMEM_SPEC] * 2,
        out_specs=VMEM_SPEC,
        compiler_params=pltpu.CompilerParams(vmem_limit_bytes=16 * 1024 * 1024),
        cost_estimate=pl.CostEstimate(flops=4_000_000_000, bytes_accessed=9_000_000, transcendentals=0),
        name="own_operand",
    )(white, jnp.asarray(spread))


GROUP = 4


def second_kernel(places, offsets, *refs):
    n = len(places)
    blocks, refs = refs[:n], refs[n:]
    (white_hbm, own_hbm, forward, inverse, picks, out_hbm, series, piece, part, full, white, own,
     grams, chosen, result, sem, near_sem, own_sem, out_sem) = refs
    copies = []
    core = offsets[SEGS]
    for i, (b, (at, part_of)) in enumerate(zip(blocks, places)):
        first, count = ((0, SHARDS), (core * 8, 8), (8 - core * 8, 8))[part_of]
        copies.append(pltpu.make_async_copy(b, series.at[at, pl.ds(first, count)], sem.at[i]))
    for c in copies:
        c.start()
    near = pltpu.make_async_copy(white_hbm, white.at[:, :, :, :, pl.ds(0, HALF)], near_sem)
    near.start()
    mine = pltpu.make_async_copy(own_hbm, own, own_sem)
    mine.start()
    for c in copies:
        c.wait()
    spectra(offsets, series, forward, piece, part, full, white, slice(HALF, SECT))
    near.wait()
    mine.wait()

    def gram(b):
        rows = own[b]
        turned = jnp.concatenate([-rows[:, HALF:], rows[:, :HALF]], axis=1)
        both = jnp.concatenate([rows, turned], axis=0)
        return dot(both, white[b].reshape(2 * HALF, SECT), NN).reshape(2, OWN, FB, SECT)

    def pair_of_blocks(b, carry):
        low, high = gram(2 * b), gram(2 * b + 1)
        for k in range(OWN):
            for ri in range(2):
                grams[k, ri, b] = jnp.concatenate([low[ri, k], high[ri, k]], axis=0).astype(BF16)
        return carry

    lax.fori_loop(0, BLOCKS // 2, pair_of_blocks, 0, unroll=8)
    outs = [
        pltpu.make_async_copy(
            result.at[pl.ds(g * GROUP, GROUP)], out_hbm.at[pl.ds(g * GROUP, GROUP)], out_sem.at[g]
        )
        for g in range(OWN // GROUP)
    ]
    for g in range(OWN // GROUP):
        for k in range(g * GROUP, (g + 1) * GROUP):
            crossed = dot(picks[k], grams[k].reshape(2 * NF, SECT), NT)
            chosen[k % GROUP] = crossed.astype(BF16)
        lags = dot(chosen[...].reshape(GROUP * NPART, 2 * NF), inverse[...], NN) * (1.0 / math.sqrt(NF))
        result[g * GROUP:(g + 1) * GROUP] = lags.reshape(GROUP, NPART, NLAG)
        outs[g].start()
    for o in outs:
        o.wait()


def second_half(offsets, blocks, places, white, own, forward, inverse, picks):
    n = len(blocks)
    return pl.pallas_call(
        functools.partial(second_kernel, places),
        out_shape=jax.ShapeDtypeStruct((OWN, NPART, NLAG), F32),
        in_specs=[SMEM_SPEC] + [ANY_SPEC] * (n + 2) + [VMEM_SPEC] * 3,
        out_specs=ANY_SPEC,
        scratch_shapes=scratch() + [
            pltpu.VMEM((BLOCKS, 2, PAIRS, 2 * FB, SECT), BF16),
            pltpu.VMEM((BLOCKS, HALF, SECT), BF16),
            pltpu.VMEM((OWN, 2, BLOCKS // 2, 2 * FB, SECT), BF16),
            pltpu.VMEM((GROUP, NPART, 2 * NF), BF16),
            pltpu.VMEM((OWN, NPART, NLAG), F32),
            pltpu.SemaphoreType.DMA((n,)),
            pltpu.SemaphoreType.DMA,
            pltpu.SemaphoreType.DMA,
            pltpu.SemaphoreType.DMA((OWN // GROUP,)),
        ],
        compiler_params=pltpu.CompilerParams(vmem_limit_bytes=34 * 1024 * 1024),
        cost_estimate=pl.CostEstimate(flops=8_000_000_000, bytes_accessed=20_000_000, transcendentals=0),
        name="far_and_cross",
    )(offsets, *blocks, white, own, forward, inverse, picks)


def per_device(record, partners, offsets):
    forward, inverse = (jnp.asarray(t) for t in build_tables())
    place = lax.axis_index("pair")
    core = place % 2
    rows = jnp.transpose(record, (1, 2, 0)).reshape(SHARDS * OWN, SHARD)
    order = np.arange(SHARD) % 128 * 4 + np.arange(SHARD) // 128
    sort = (np.arange(SHARD)[:, None] == order[None, :]).astype(jnp.bfloat16)
    rows = jnp.dot(rows, jnp.asarray(sort), preferred_element_type=BF16)
    mine = lax.all_to_all(
        rows.reshape(SHARDS, OWN, SHARD), "tm", split_axis=0, concat_axis=0, tiled=True
    )

    onward = [(i, (i + 2 - 4 * (i % 2)) % 16) for i in range(16)]
    across = [(i, i ^ 1) for i in range(16)]

    def send(v, pairs):
        return lax.ppermute(v, "pair", pairs)

    def half(v):
        return lax.dynamic_slice_in_dim(v, core * 8, 8, 0)

    tie = lax.optimization_barrier
    other = send(mine, across)
    m1, o1 = send(mine, onward), send(other, onward)
    m2, o2 = send(m1, onward), send(o1, onward)
    xm1, xo1 = send(m1, across), send(o1, across)
    m3, o3 = send(m2, onward), send(o2, onward)
    xm2, xo2 = send(m2, across), send(o2, across)
    near = [mine, other, m1, o1, xm1, xo1, m2, o2]
    numbers = jnp.concatenate([offsets, core[None]])
    white = near_spectra(numbers, near, forward)
    m3, o3, white = tie((m3, o3, white))
    m4, o4 = send(half(m3), onward), send(half(o3), onward)
    xm3, xo3 = send(m3, across), send(o3, across)
    own = own_operand(white)
    m4, o4, own = tie((m4, o4, own))
    xm4, xo4 = send(m4, across), send(o4, across)

    far = [xm2, xo2, m3, o3, xm3, xo3, m4, xo4, o4, xm4]
    places = [(i, 0) for i in range(6)] + [(6, 1), (6, 2), (7, 1), (7, 2)]

    toward = 2 * (2 * core - 1)
    steps = np.array([0, 0, 1, 1, -1, -1, 2, 2, -2, -2, 3, 3, -3, -3, 4, 4], np.int32)
    swap = np.array([0, 1, 0, 1, 1, 0, 0, 1, 1, 0, 0, 1, 1, 0, 0, 1], np.int32)
    origin = ((place + toward * steps) % 16) ^ swap
    channel = jnp.repeat(origin * OWN, OWN) + np.tile(np.arange(OWN, dtype=np.int32), 16)
    picks = ((partners % SECT)[:, :, None] == channel).astype(BF16)
    return second_half(numbers, far, places, white, own, forward, inverse, picks)


def solution(mesh):
    in_specs = (P("tm", None, "pair"), P(("tm", "pair"), None), P())
    out_specs = P(("tm", "pair"), None, None)
    return jax.shard_map(
        per_device, mesh=mesh, in_specs=in_specs, out_specs=out_specs, check_vma=False
    )
```

time: 115 us -> 76.8 us (0.67)
  waiting for transfers between devices: 40.7 us -> 7.04 us
  starting transfers between devices: 0.01 us -> 24.5 us
  Pallas kernels: 43.1 us -> 22.9 us
  between operations: 13.4 us -> 0.35 us
  local copies, waits for them, and re-layouts: 0 us -> 5.17 us
  other arithmetic: 2.47 us -> 0.37 us
  matrix products: 0 us -> 1.33 us
    all_gather x1 -> x0, waiting for transfers between devices: 40.7 us -> none  [per_device(): series = lax.all_gather(mine, 'pair', axis=0)]
    ppermute x0 -> x17, starting transfers between devices: none -> 24.5 us  [send(): return lax.ppermute(v, 'pair', pairs)]
    pallas_call x1 -> x3, Pallas kernels: 43.1 us -> 22.9 us  [the longest x1 14.9 us: second_half(): pl.pallas_call(functools.partial(second_kernel, places), out_shape=jax.Sh...]
    ppermute x0 -> x17, waiting for transfers between devices: none -> 7.04 us  [send(): return lax.ppermute(v, 'pair', pairs)]
    unnamed x0 -> x24, local copies, waits for them, and re-layouts: none -> 5.07 us
    convert_element_type x2 -> x1, other arithmetic: 1.75 us -> 0.2 us  [per_device(): picks = ((partners % SECT)[:, :, None] == channel).astype(BF16)]
    dot_general x0 -> x1, matrix products: none -> 1.33 us  [per_device(): rows = jnp.dot(rows, jnp.asarray(sort), preferred_element_type=BF16)]
  transfers between devices with their start and end apart: 1 -> 17, of which waited for: 1 -> 6; matrix products, arithmetic and copies ran while one was open for 2% -> 1% of each run, Pallas kernels for 0% -> 10%
where the time goes in v1:
time: 76.8 us; the launch traced here: 76.6 us
  starting transfers between devices  24.5 us (32%)
  Pallas kernels  22.9 us (30%)
  blocking collectives  14.9 us (19%)
  waiting for transfers between devices  7.04 us (9%)
  local copies, waits for them, and re-layouts  5.17 us (7%)
  matrix products  1.33 us (2%)
    ppermute x17, starting transfers between devices, send(): return lax.ppermute(v, 'pair', pairs)  24.5 us
    all_to_all x1, blocking collectives, per_device(): lax.all_to_all(rows.reshape(SHARDS, OWN, SHARD), 'tm', split_axis=0, conc...  14.9 us
    pallas_call x1, Pallas kernels, second_half(): pl.pallas_call(functools.partial(second_kernel, places), out_shape=jax.Sh...  14.9 us
    ppermute x17, waiting for transfers between devices, send(): return lax.ppermute(v, 'pair', pairs)  7.04 us
    pallas_call x1, Pallas kernels, near_spectra(): pl.pallas_call(near_kernel, out_shape=jax.ShapeDtypeStruct((BLOCKS, 2, PA...  5.55 us
    unnamed x24, local copies, waits for them, and re-layouts  5.07 us
    pallas_call x1, Pallas kernels, own_operand(): pl.pallas_call(own_kernel, out_shape=jax.ShapeDtypeStruct((BLOCKS, HALF,...  2.44 us
  transfers between devices with their start and end apart: 17, of which 6 were waited for; matrix products, arithmetic and copies ran while one was open for 1% of the time, Pallas kernels for 10%

profile of v1, /device:TPU:1, one launch (start us, length us, event | category | flops | bytes accessed | tf_op | source)
XLA Modules:
  0.0 76.6 jit_solution(5650512248528214986)
XLA Ops:
  0.0 0.0 copy-start.8
  0.0 0.0 copy-start.2
  0.0 0.9 %copy-done = bf16[512,16,16]{0,2,1:T(8,128)(2,1)S(1)} copy-done((bf16[512,16,16]{0,2,1:T(8,128)(2,1)S(1)}, bf16[512,16,16]{0,2,1:T(8,128)(2,1)}, u32[]{:S(2)}) %copy-start) | copy-done | bytes 262168
  1.0 1.3 %convolution_bitcast_fusion = bf16[16,16,512]{2,1,0:T(8,128)(2,1)S(1)} fusion(bf16[512,512,1]{1,0,2:T(8,128)(2,1)} %constant.75, bf16[512,16,16]{0,2,1:T(8,128)(2,1)S(1)} %copy-done), kind=kOutput, calls=%fused_computation | convolution fusion | flops 134217728 | bytes 1048576 | tf_op jit(solution)/shard_map/dot_general | solution.py:282
  2.3 14.9 %all_to_all.5.refs_0_ = bf16[16,16,512]{2,1,0:T(8,128)(2,1)S(1)} all-to-all(bf16[16,16,512]{2,1,0:T(8,128)(2,1)S(1)} %convolution_bitcast_fusion), channel_id=1, replica_groups=mesh['tm'=16,'pair'=16] {'tm'}, dimensions={0} | all-to-all | bytes 524288 | tf_op jit(solution)/shard_map/all_to_all | solution.py:283
  17.2 2.1 %collective-permute-start.3 = (bf16[16,16,512]{2,1,0:T(8,128)(2,1)S(1)}, bf16[16,16,512]{2,1,0:T(8,128)(2,1)S(1)}, u32[]{:S(2)}, u32[]{:S(2)}) collective-permute-start(bf16[16,16,512]{2,1,0:T(8,128)(2,1)S(1)} %all_to_all.5.refs_0_), channel_id=1, source_target_pairs={{0,1},{1,0},{2,3},{3,2},{4,5},{5,4},{6,7},{7,6},{8,9},{9,8},{10,11... | collective-permute-start | bytes 786440 | tf_op jit(solution)/shard_map/ppermute | solution.py:291
  19.3 5.6 %collective-permute-start = (bf16[16,16,512]{2,1,0:T(8,128)(2,1)S(1)}, bf16[16,16,512]{2,1,0:T(8,128)(2,1)S(1)}, u32[]{:S(2)}, u32[]{:S(2)}) collective-permute-start(bf16[16,16,512]{2,1,0:T(8,128)(2,1)S(1)} %all_to_all.5.refs_0_), channel_id=1, source_target_pairs={{0,2},{1,15},{2,4},{3,1},{4,6},{5,3},{6,8},{7,5},{8,10},{9,7},{10,... | collective-permute-start | bytes 786440 | tf_op jit(solution)/shard_map/ppermute | solution.py:291
  24.9 0.0 collective-permute-done.3.refs_1_
  24.9 1.2 %collective-permute-start.4 = (bf16[16,16,512]{2,1,0:T(8,128)(2,1)S(1)}, bf16[16,16,512]{2,1,0:T(8,128)(2,1)S(1)}, u32[]{:S(2)}, u32[]{:S(2)}) collective-permute-start(bf16[16,16,512]{2,1,0:T(8,128)(2,1)S(1)} %collective-permute-done.3.refs_1_), channel_id=1, source_target_pairs={{0,2},{1,15},{2,4},{3,1},{4,6},{5,3},{6,8},{7,5},{8,10},{9,7},{10,... | collective-permute-start | bytes 786440 | tf_op jit(solution)/shard_map/ppermute | solution.py:291
  26.1 2.1 %collective-permute-done.refs_2_ = bf16[16,16,512]{2,1,0:T(8,128)(2,1)S(1)} collective-permute-done((bf16[16,16,512]{2,1,0:T(8,128)(2,1)S(1)}, bf16[16,16,512]{2,1,0:T(8,128)(2,1)S(1)}, u32[]{:S(2)}, u32[]{:S(2)}) %collective-permute-start) | collective-permute-done | bytes 262176 | tf_op jit(solution)/shard_map/ppermute | solution.py:291
  28.2 1.3 %collective-permute-start.9 = (bf16[16,16,512]{2,1,0:T(8,128)(2,1)S(1)}, bf16[16,16,512]{2,1,0:T(8,128)(2,1)S(1)}, u32[]{:S(2)}, u32[]{:S(2)}) collective-permute-start(bf16[16,16,512]{2,1,0:T(8,128)(2,1)S(1)} %collective-permute-done.refs_2_), channel_id=1, source_target_pairs={{0,1},{1,0},{2,3},{3,2},{4,5},{5,4},{6,7},{7,6},{8,9},{9,8},{10,11... | collective-permute-start | bytes 786440 | tf_op jit(solution)/shard_map/ppermute | solution.py:291
  29.5 1.8 %collective-permute-start.1 = (bf16[16,16,512]{2,1,0:T(8,128)(2,1)S(1)}, bf16[16,16,512]{2,1,0:T(8,128)(2,1)S(1)}, u32[]{:S(2)}, u32[]{:S(2)}) collective-permute-start(bf16[16,16,512]{2,1,0:T(8,128)(2,1)S(1)} %collective-permute-done.refs_2_), channel_id=1, source_target_pairs={{0,2},{1,15},{2,4},{3,1},{4,6},{5,3},{6,8},{7,5},{8,10},{9,7},{10,... | collective-permute-start | bytes 786440 | tf_op jit(solution)/shard_map/ppermute | solution.py:291
  31.3 0.0 collective-permute-done.4.refs_3_
  31.3 1.0 %collective-permute-start.10 = (bf16[16,16,512]{2,1,0:T(8,128)(2,1)S(1)}, bf16[16,16,512]{2,1,0:T(8,128)(2,1)S(1)}, u32[]{:S(2)}, u32[]{:S(2)}) collective-permute-start(bf16[16,16,512]{2,1,0:T(8,128)(2,1)S(1)} %collective-permute-done.4.refs_3_), channel_id=1, source_target_pairs={{0,1},{1,0},{2,3},{3,2},{4,5},{5,4},{6,7},{7,6},{8,9},{9,8},{10,11... | collective-permute-start | bytes 786440 | tf_op jit(solution)/shard_map/ppermute | solution.py:291
  32.3 1.8 %collective-permute-start.5 = (bf16[16,16,512]{2,1,0:T(8,128)(2,1)S(1)}, bf16[16,16,512]{2,1,0:T(8,128)(2,1)S(1)}, u32[]{:S(2)}, u32[]{:S(2)}) collective-permute-start(bf16[16,16,512]{2,1,0:T(8,128)(2,1)S(1)} %collective-permute-done.4.refs_3_), channel_id=1, source_target_pairs={{0,2},{1,15},{2,4},{3,1},{4,6},{5,3},{6,8},{7,5},{8,10},{9,7},{10,... | collective-permute-start | bytes 786440 | tf_op jit(solution)/shard_map/ppermute | solution.py:291
  34.2 0.1 pad_add_fusion.offsets
  34.2 0.1 broadcast_add_fusion
  34.3 0.7 collective-permute-done.1.refs_6_
  35.1 2.7 %collective-permute-start.7 = (bf16[16,16,512]{2,1,0:T(8,128)(2,1)S(1)}, bf16[16,16,512]{2,1,0:T(8,128)(2,1)S(1)}, u32[]{:S(2)}, u32[]{:S(2)}) collective-permute-start(bf16[16,16,512]{2,1,0:T(8,128)(2,1)S(1)} %collective-permute-done.1.refs_6_), channel_id=1, source_target_pairs={{0,2},{1,15},{2,4},{3,1},{4,6},{5,3},{6,8},{7,5},{8,10},{9,7},{10,... | collective-permute-start | bytes 786440 | tf_op jit(solution)/shard_map/ppermute | solution.py:291
  37.8 0.1 collective-permute-done.5.refs_7_
  37.9 2.7 %collective-permute-start.8 = (bf16[16,16,512]{2,1,0:T(8,128)(2,1)S(1)}, bf16[16,16,512]{2,1,0:T(8,128)(2,1)S(1)}, u32[]{:S(2)}, u32[]{:S(2)}) collective-permute-start(bf16[16,16,512]{2,1,0:T(8,128)(2,1)S(1)} %collective-permute-done.5.refs_7_), channel_id=1, source_target_pairs={{0,2},{1,15},{2,4},{3,1},{4,6},{5,3},{6,8},{7,5},{8,10},{9,7},{10,... | collective-permute-start | bytes 786440 | tf_op jit(solution)/shard_map/ppermute | solution.py:291
  40.6 0.0 collective-permute-done.9.refs_4_
  40.6 0.0 collective-permute-done.10.refs_5_
  40.6 5.5 %near_spectra.1.white.refs_10_ = bf16[64,2,8,16,128]{4,3,2,1,0:T(8,128)(2,1)S(1)} custom-call(s32[16]{0:T(128)S(1)} %pad_add_fusion.offsets, bf16[16,16,512]{2,1,0:T(8,128)(2,1)S(1)} %all_to_all.5.refs_0_, bf16[16,16,512]{2,1,0:T(8,128)(2,1)S(1)} %collective-permute-done.3.refs_1_, bf16[16,16,512]{2,1,0:T(8,128)(2,1)S(1)} %collective-permute-done.refs_2_, ...), custom_call_target="tpu_custom_call" | custom-call | flops 5000000000 | bytes 7000000 | tf_op jit(solution)/shard_map/near_spectra/pallas_call | solution.py:170
  46.2 1.9 %copy-done.4 = bf16[64,2,8,16,128]{4,3,2,1,0:T(8,128)(2,1)} copy-done((bf16[64,2,8,16,128]{4,3,2,1,0:T(8,128)(2,1)}, bf16[64,2,8,16,128]{4,3,2,1,0:T(8,128)(2,1)S(1)}, u32[]{:S(2)}) %copy-start.4) | copy-done | bytes 4194328
  48.1 0.0 collective-permute-done.7.refs_2_
  48.1 0.0 collective-permute-done.8.refs_3_
  48.1 0.3 collective-permute-start.14
  48.4 0.1 reshape.11
  48.5 0.0 collective-permute-start.2
  48.5 0.5 collective-permute-start.6
  49.0 0.1 collective-permute-start.12
  49.1 0.4 collective-permute-start.11
  49.6 0.0 copy-start.1
  49.6 2.9 %collective-permute-done.14.refs_8_ = bf16[8,16,512]{2,1,0:T(8,128)(2,1)S(1)} collective-permute-done((bf16[8,16,512]{2,1,0:T(8,128)(2,1)S(1)}, bf16[8,16,512]{2,1,0:T(8,128)(2,1)S(1)}, u32[]{:S(2)}, u32[]{:S(2)}) %collective-permute-start.14) | collective-permute-done | bytes 131104 | tf_op jit(solution)/shard_map/ppermute | solution.py:291
  52.5 0.9 %collective-permute-start.13 = (bf16[8,16,512]{2,1,0:T(8,128)(2,1)S(1)}, bf16[8,16,512]{2,1,0:T(8,128)(2,1)S(1)}, u32[]{:S(2)}, u32[]{:S(2)}) collective-permute-start(bf16[8,16,512]{2,1,0:T(8,128)(2,1)S(1)} %constant_dynamic-slice_fusion.1), channel_id=1, source_target_pairs={{0,2},{1,15},{2,4},{3,1},{4,6},{5,3},{6,8},{7,5},{8,10},{9,7},{10,... | collective-permute-start | bytes 393224 | tf_op jit(solution)/shard_map/ppermute | solution.py:291
  53.4 2.2 %copy-done.5 = bf16[64,2,8,16,128]{4,3,2,1,0:T(8,128)(2,1)S(1)} copy-done((bf16[64,2,8,16,128]{4,3,2,1,0:T(8,128)(2,1)S(1)}, bf16[64,2,8,16,128]{4,3,2,1,0:T(8,128)(2,1)}, u32[]{:S(2)}) %copy-start.5) | copy-done | bytes 4194328
  55.6 2.4 %own_operand.1.refs_11_ = bf16[64,128,256]{2,1,0:T(8,128)(2,1)S(1)} custom-call(bf16[64,2,8,16,128]{4,3,2,1,0:T(8,128)(2,1)S(1)} %copy-done.5, bf16[128,128]{1,0:T(8,128)(2,1)S(1)} %copy-done.3), custom_call_target="tpu_custom_call" | custom-call | flops 4000000000 | bytes 9000000 | tf_op jit(solution)/shard_map/own_operand/pallas_call | solution.py:184
  58.1 0.0 collective-permute-done.13.refs_6_
  58.1 2.1 %collective-permute-start.16 = (bf16[8,16,512]{2,1,0:T(8,128)(2,1)S(1)}, bf16[8,16,512]{2,1,0:T(8,128)(2,1)S(1)}, u32[]{:S(2)}, u32[]{:S(2)}) collective-permute-start(bf16[8,16,512]{2,1,0:T(8,128)(2,1)S(1)} %collective-permute-done.13.refs_6_), channel_id=1, source_target_pairs={{0,1},{1,0},{2,3},{3,2},{4,5},{5,4},{6,7},{7,6},{8,9},{9,8},{10,11... | collective-permute-start | bytes 393224 | tf_op jit(solution)/shard_map/ppermute | solution.py:291
  60.1 0.0 collective-permute-done.2.refs_0_
  60.1 0.0 collective-permute-start.15
  60.2 0.2 compare_convert_fusion.refs_14_
  60.4 0.8 collective-permute-done.16.refs_9_
  61.1 0.4 collective-permute-done.15.refs_7_
  61.5 0.0 collective-permute-done.11.refs_4_
  61.5 0.0 collective-permute-done.12.refs_5_
  61.5 14.9 %far_and_cross.1 = f32[16,64,512]{2,1,0:T(8,128)} custom-call(s32[16]{0:T(128)S(1)} %pad_add_fusion.offsets, bf16[16,16,512]{2,1,0:T(8,128)(2,1)S(1)} %collective-permute-done.2.refs_0_, bf16[16,16,512]{2,1,0:T(8,128)(2,1)S(1)} %collective-permute-done.6.refs_1_, bf16[16,16,512]{2,1,0:T(8,128)(2,1)S(1)} %collective-permute-done.7.refs_2_, ...), custom_call_target="tpu_custom_call" | custom-call | flops 8000000000 | bytes 20000000 | tf_op jit(solution)/shard_map/far_and_cross/pallas_call | solution.py:253
  (23 shorter events, 0.1 us)
Async XLA Ops:
  0.0 1.0 %copy-start = (bf16[512,16,16]{0,2,1:T(8,128)(2,1)S(1)}, bf16[512,16,16]{0,2,1:T(8,128)(2,1)}, u32[]{:S(2)}) copy-start(bf16[512,16,16]{0,2,1:T(8,128)(2,1)} %param.10) | copy-start | bytes 786436
  0.0 26.1 %copy-start.9 = (s32[16]{0:T(128)S(1)}, s32[16]{0:T(128)}, u32[]{:S(2)}) copy-start(s32[16]{0:T(128)} %constant.71.clone) | copy-start | bytes 196
  0.0 26.1 %copy-start.10 = (s32[16]{0:T(128)S(1)}, s32[16]{0:T(128)}, u32[]{:S(2)}) copy-start(s32[16]{0:T(128)} %constant.70.clone) | copy-start | bytes 196
  0.0 34.2 %copy-start.8 = (s32[16,16]{1,0:T(8,128)S(1)}, s32[16,16]{1,0:T(8,128)}, u32[]{:S(2)}) copy-start(s32[16,16]{1,0:T(8,128)} %constant.74) | copy-start | bytes 3076
  0.0 40.6 %copy-start.2 = (bf16[4,256,256]{2,1,0:T(8,128)(2,1)S(1)}, bf16[4,256,256]{2,1,0:T(8,128)(2,1)}, u32[]{:S(2)}) copy-start(bf16[4,256,256]{2,1,0:T(8,128)(2,1)} %constant.66.clone.refs_8_.refs_12_) | copy-start | bytes 1572868
  0.0 34.1 %copy-start.11 = (s32[15]{0:T(128)S(1)}, s32[15]{0:T(128)}, u32[]{:S(2)}) copy-start(s32[15]{0:T(128)} %param.12) | copy-start | bytes 184
  17.2 7.7 %collective-permute-start.3 = (bf16[16,16,512]{2,1,0:T(8,128)(2,1)S(1)}, bf16[16,16,512]{2,1,0:T(8,128)(2,1)S(1)}, u32[]{:S(2)}, u32[]{:S(2)}) collective-permute-start(bf16[16,16,512]{2,1,0:T(8,128)(2,1)S(1)} %all_to_all.5.refs_0_), channel_id=1, source_target_pairs={{0,1},{1,0},{2,3},{3,2},{4,5},{5,4},{6,7},{7,6},{8,9},{9,8},{10,11... | collective-permute-start | bytes 786440 | tf_op jit(solution)/shard_map/ppermute | solution.py:291
  19.3 8.9 %collective-permute-start = (bf16[16,16,512]{2,1,0:T(8,128)(2,1)S(1)}, bf16[16,16,512]{2,1,0:T(8,128)(2,1)S(1)}, u32[]{:S(2)}, u32[]{:S(2)}) collective-permute-start(bf16[16,16,512]{2,1,0:T(8,128)(2,1)S(1)} %all_to_all.5.refs_0_), channel_id=1, source_target_pairs={{0,2},{1,15},{2,4},{3,1},{4,6},{5,3},{6,8},{7,5},{8,10},{9,7},{10,... | collective-permute-start | bytes 786440 | tf_op jit(solution)/shard_map/ppermute | solution.py:291
  24.9 6.4 %collective-permute-start.4 = (bf16[16,16,512]{2,1,0:T(8,128)(2,1)S(1)}, bf16[16,16,512]{2,1,0:T(8,128)(2,1)S(1)}, u32[]{:S(2)}, u32[]{:S(2)}) collective-permute-start(bf16[16,16,512]{2,1,0:T(8,128)(2,1)S(1)} %collective-permute-done.3.refs_1_), channel_id=1, source_target_pairs={{0,2},{1,15},{2,4},{3,1},{4,6},{5,3},{6,8},{7,5},{8,10},{9,7},{10,... | collective-permute-start | bytes 786440 | tf_op jit(solution)/shard_map/ppermute | solution.py:291
  28.2 12.4 %collective-permute-start.9 = (bf16[16,16,512]{2,1,0:T(8,128)(2,1)S(1)}, bf16[16,16,512]{2,1,0:T(8,128)(2,1)S(1)}, u32[]{:S(2)}, u32[]{:S(2)}) collective-permute-start(bf16[16,16,512]{2,1,0:T(8,128)(2,1)S(1)} %collective-permute-done.refs_2_), channel_id=1, source_target_pairs={{0,1},{1,0},{2,3},{3,2},{4,5},{5,4},{6,7},{7,6},{8,9},{9,8},{10,11... | collective-permute-start | bytes 786440 | tf_op jit(solution)/shard_map/ppermute | solution.py:291
  29.5 5.5 %collective-permute-start.1 = (bf16[16,16,512]{2,1,0:T(8,128)(2,1)S(1)}, bf16[16,16,512]{2,1,0:T(8,128)(2,1)S(1)}, u32[]{:S(2)}, u32[]{:S(2)}) collective-permute-start(bf16[16,16,512]{2,1,0:T(8,128)(2,1)S(1)} %collective-permute-done.refs_2_), channel_id=1, source_target_pairs={{0,2},{1,15},{2,4},{3,1},{4,6},{5,3},{6,8},{7,5},{8,10},{9,7},{10,... | collective-permute-start | bytes 786440 | tf_op jit(solution)/shard_map/ppermute | solution.py:291
  31.3 9.2 %collective-permute-start.10 = (bf16[16,16,512]{2,1,0:T(8,128)(2,1)S(1)}, bf16[16,16,512]{2,1,0:T(8,128)(2,1)S(1)}, u32[]{:S(2)}, u32[]{:S(2)}) collective-permute-start(bf16[16,16,512]{2,1,0:T(8,128)(2,1)S(1)} %collective-permute-done.4.refs_3_), channel_id=1, source_target_pairs={{0,1},{1,0},{2,3},{3,2},{4,5},{5,4},{6,7},{7,6},{8,9},{9,8},{10,11... | collective-permute-start | bytes 786440 | tf_op jit(solution)/shard_map/ppermute | solution.py:291
  32.3 5.5 %collective-permute-start.5 = (bf16[16,16,512]{2,1,0:T(8,128)(2,1)S(1)}, bf16[16,16,512]{2,1,0:T(8,128)(2,1)S(1)}, u32[]{:S(2)}, u32[]{:S(2)}) collective-permute-start(bf16[16,16,512]{2,1,0:T(8,128)(2,1)S(1)} %collective-permute-done.4.refs_3_), channel_id=1, source_target_pairs={{0,2},{1,15},{2,4},{3,1},{4,6},{5,3},{6,8},{7,5},{8,10},{9,7},{10,... | collective-permute-start | bytes 786440 | tf_op jit(solution)/shard_map/ppermute | solution.py:291
  34.3 14.1 %copy-start.7 = (s32[16,64]{1,0:T(8,128)S(1)}, s32[16,64]{1,0:T(8,128)}, u32[]{:S(2)}) copy-start(s32[16,64]{1,0:T(8,128)} %param.11) | copy-start | bytes 12292
  34.3 19.1 %copy-start.3 = (bf16[128,128]{1,0:T(8,128)(2,1)S(1)}, bf16[128,128]{1,0:T(8,128)(2,1)}, u32[]{:S(2)}) copy-start(bf16[128,128]{1,0:T(8,128)(2,1)} %constant.69.clone.spread) | copy-start | bytes 98308
  35.1 13.0 %collective-permute-start.7 = (bf16[16,16,512]{2,1,0:T(8,128)(2,1)S(1)}, bf16[16,16,512]{2,1,0:T(8,128)(2,1)S(1)}, u32[]{:S(2)}, u32[]{:S(2)}) collective-permute-start(bf16[16,16,512]{2,1,0:T(8,128)(2,1)S(1)} %collective-permute-done.1.refs_6_), channel_id=1, source_target_pairs={{0,2},{1,15},{2,4},{3,1},{4,6},{5,3},{6,8},{7,5},{8,10},{9,7},{10,... | collective-permute-start | bytes 786440 | tf_op jit(solution)/shard_map/ppermute | solution.py:291
  37.9 10.2 %collective-permute-start.8 = (bf16[16,16,512]{2,1,0:T(8,128)(2,1)S(1)}, bf16[16,16,512]{2,1,0:T(8,128)(2,1)S(1)}, u32[]{:S(2)}, u32[]{:S(2)}) collective-permute-start(bf16[16,16,512]{2,1,0:T(8,128)(2,1)S(1)} %collective-permute-done.5.refs_7_), channel_id=1, source_target_pairs={{0,2},{1,15},{2,4},{3,1},{4,6},{5,3},{6,8},{7,5},{8,10},{9,7},{10,... | collective-permute-start | bytes 786440 | tf_op jit(solution)/shard_map/ppermute | solution.py:291
  46.2 1.9 %copy-start.4 = (bf16[64,2,8,16,128]{4,3,2,1,0:T(8,128)(2,1)}, bf16[64,2,8,16,128]{4,3,2,1,0:T(8,128)(2,1)S(1)}, u32[]{:S(2)}) copy-start(bf16[64,2,8,16,128]{4,3,2,1,0:T(8,128)(2,1)S(1)} %near_spectra.1.white.refs_10_) | copy-start | bytes 12582916
  48.1 4.4 %collective-permute-start.14 = (bf16[8,16,512]{2,1,0:T(8,128)(2,1)S(1)}, bf16[8,16,512]{2,1,0:T(8,128)(2,1)S(1)}, u32[]{:S(2)}, u32[]{:S(2)}) collective-permute-start(bf16[8,16,512]{2,1,0:T(8,128)(2,1)S(1)} %constant_dynamic-slice_fusion), channel_id=1, source_target_pairs={{0,2},{1,15},{2,4},{3,1},{4,6},{5,3},{6,8},{7,5},{8,10},{9,7},{10,... | collective-permute-start | bytes 393224 | tf_op jit(solution)/shard_map/ppermute | solution.py:291
  48.5 11.6 %collective-permute-start.2 = (bf16[16,16,512]{2,1,0:T(8,128)(2,1)S(1)}, bf16[16,16,512]{2,1,0:T(8,128)(2,1)S(1)}, u32[]{:S(2)}, u32[]{:S(2)}) collective-permute-start(bf16[16,16,512]{2,1,0:T(8,128)(2,1)S(1)} %collective-permute-done.1.refs_6_), channel_id=1, source_target_pairs={{0,1},{1,0},{2,3},{3,2},{4,5},{5,4},{6,7},{7,6},{8,9},{9,8},{10,11... | collective-permute-start | bytes 786440 | tf_op jit(solution)/shard_map/ppermute | solution.py:291
  48.5 11.8 %collective-permute-start.6 = (bf16[16,16,512]{2,1,0:T(8,128)(2,1)S(1)}, bf16[16,16,512]{2,1,0:T(8,128)(2,1)S(1)}, u32[]{:S(2)}, u32[]{:S(2)}) collective-permute-start(bf16[16,16,512]{2,1,0:T(8,128)(2,1)S(1)} %collective-permute-done.5.refs_7_), channel_id=1, source_target_pairs={{0,1},{1,0},{2,3},{3,2},{4,5},{5,4},{6,7},{7,6},{8,9},{9,8},{10,11... | collective-permute-start | bytes 786440 | tf_op jit(solution)/shard_map/ppermute | solution.py:291
  49.0 12.5 %collective-permute-start.12 = (bf16[16,16,512]{2,1,0:T(8,128)(2,1)S(1)}, bf16[16,16,512]{2,1,0:T(8,128)(2,1)S(1)}, u32[]{:S(2)}, u32[]{:S(2)}) collective-permute-start(bf16[16,16,512]{2,1,0:T(8,128)(2,1)S(1)} %collective-permute-done.8.refs_3_), channel_id=1, source_target_pairs={{0,1},{1,0},{2,3},{3,2},{4,5},{5,4},{6,7},{7,6},{8,9},{9,8},{10,11... | collective-permute-start | bytes 786440 | tf_op jit(solution)/shard_map/ppermute | solution.py:291
  49.1 12.4 %collective-permute-start.11 = (bf16[16,16,512]{2,1,0:T(8,128)(2,1)S(1)}, bf16[16,16,512]{2,1,0:T(8,128)(2,1)S(1)}, u32[]{:S(2)}, u32[]{:S(2)}) collective-permute-start(bf16[16,16,512]{2,1,0:T(8,128)(2,1)S(1)} %collective-permute-done.7.refs_2_), channel_id=1, source_target_pairs={{0,1},{1,0},{2,3},{3,2},{4,5},{5,4},{6,7},{7,6},{8,9},{9,8},{10,11... | collective-permute-start | bytes 786440 | tf_op jit(solution)/shard_map/ppermute | solution.py:291
  49.6 11.9 %copy-start.1 = (bf16[1024,512]{1,0:T(8,128)(2,1)S(1)}, bf16[1024,512]{1,0:T(8,128)(2,1)}, u32[]{:S(2)}) copy-start(bf16[1024,512]{1,0:T(8,128)(2,1)} %constant.67.clone.refs_13_) | copy-start | bytes 3145732
  52.5 5.6 %collective-permute-start.13 = (bf16[8,16,512]{2,1,0:T(8,128)(2,1)S(1)}, bf16[8,16,512]{2,1,0:T(8,128)(2,1)S(1)}, u32[]{:S(2)}, u32[]{:S(2)}) collective-permute-start(bf16[8,16,512]{2,1,0:T(8,128)(2,1)S(1)} %constant_dynamic-slice_fusion.1), channel_id=1, source_target_pairs={{0,2},{1,15},{2,4},{3,1},{4,6},{5,3},{6,8},{7,5},{8,10},{9,7},{10,... | collective-permute-start | bytes 393224 | tf_op jit(solution)/shard_map/ppermute | solution.py:291
  53.4 2.2 %copy-start.5 = (bf16[64,2,8,16,128]{4,3,2,1,0:T(8,128)(2,1)S(1)}, bf16[64,2,8,16,128]{4,3,2,1,0:T(8,128)(2,1)}, u32[]{:S(2)}) copy-start(bf16[64,2,8,16,128]{4,3,2,1,0:T(8,128)(2,1)} %copy-done.4) | copy-start | bytes 12582916
  55.6 5.9 %copy-start.6 = (bf16[64,2,8,16,128]{4,3,2,1,0:T(8,128)(2,1)S(1)}, bf16[64,2,8,16,128]{4,3,2,1,0:T(8,128)(2,1)}, u32[]{:S(2)}) copy-start(bf16[64,2,8,16,128]{4,3,2,1,0:T(8,128)(2,1)} %copy-done.4) | copy-start | bytes 12582916
  58.1 3.1 %collective-permute-start.16 = (bf16[8,16,512]{2,1,0:T(8,128)(2,1)S(1)}, bf16[8,16,512]{2,1,0:T(8,128)(2,1)S(1)}, u32[]{:S(2)}, u32[]{:S(2)}) collective-permute-start(bf16[8,16,512]{2,1,0:T(8,128)(2,1)S(1)} %collective-permute-done.13.refs_6_), channel_id=1, source_target_pairs={{0,1},{1,0},{2,3},{3,2},{4,5},{5,4},{6,7},{7,6},{8,9},{9,8},{10,11... | collective-permute-start | bytes 393224 | tf_op jit(solution)/shard_map/ppermute | solution.py:291
  60.1 1.3 %collective-permute-start.15 = (bf16[8,16,512]{2,1,0:T(8,128)(2,1)S(1)}, bf16[8,16,512]{2,1,0:T(8,128)(2,1)S(1)}, u32[]{:S(2)}, u32[]{:S(2)}) collective-permute-start(bf16[8,16,512]{2,1,0:T(8,128)(2,1)S(1)} %collective-permute-done.14.refs_8_), channel_id=1, source_target_pairs={{0,1},{1,0},{2,3},{3,2},{4,5},{5,4},{6,7},{7,6},{8,9},{9,8},{10,11... | collective-permute-start | bytes 393224 | tf_op jit(solution)/shard_map/ppermute | solution.py:291

commit v2 on v1

--- a/solution.py
+++ b/solution.py
@@ -120,26 +120,33 @@
                 ).astype(BF16)
 
 
-def spectra(offsets, series, forward, piece, part, full, white, lanes):
+def spectra(offsets, series, forward, piece, part, full, white, lanes, after=lambda u: None):
     cut_pieces(offsets, series, piece, 0, 0)
     for u in range(PAIRS):
         transform(forward, piece, part, u % 2)
         if u + 1 < PAIRS:
             cut_pieces(offsets, series, piece, u + 1, (u + 1) % 2)
         whiten(part, full.at[u % 2], white, u, u % 2, lanes)
+        after(u)
 
 
 def near_kernel(offsets, *refs):
-    blocks, (forward, white, series, piece, part, full, sem) = refs[:8], refs[8:]
+    blocks, refs = refs[:8], refs[8:]
+    (forward, spread, white_hbm, own_hbm, token, white, own, series, piece, part, full, sem, near_sem,
+     own_sem) = refs
     copies = [pltpu.make_async_copy(b, series.at[i], sem.at[i]) for i, b in enumerate(blocks)]
     for c in copies:
         c.start()
     for c in copies:
         c.wait()
-    spectra(offsets, series, forward, piece, part, full, white, slice(0, HALF))
-
-
-def own_kernel(white, spread, own):
+    kept = [
+        pltpu.make_async_copy(white.at[:, :, u], white_hbm.at[:, :, u], near_sem.at[u])
+        for u in range(PAIRS)
+    ]
+    spectra(
+        offsets, series, forward, piece, part, full, white, slice(0, HALF), lambda u: kept[u].start()
+    )
+    token[...] = jnp.zeros((8, 128), F32)
     row = lax.broadcasted_iota(jnp.int32, (HALF, 2 * HALF), 0)
     column = lax.broadcasted_iota(jnp.int32, (HALF, 2 * HALF), 1)
     mask = (row % FB == column % FB) & (column % HALF < SEGS * FB)
@@ -149,7 +156,16 @@
         own[b] = jnp.where(mask, spreaded, 0.0).astype(BF16)
         return carry
 
-    lax.fori_loop(0, BLOCKS, rows, 0, unroll=8)
+    outs = []
+    for i in range(CUTS):
+        cut = pl.ds(i * (BLOCKS // CUTS), BLOCKS // CUTS)
+        lax.fori_loop(i * (BLOCKS // CUTS), (i + 1) * (BLOCKS // CUTS), rows, 0, unroll=8)
+        outs.append(pltpu.make_async_copy(own.at[cut], own_hbm.at[cut], own_sem.at[i]))
+        outs[-1].start()
+    for o in outs:
+        o.wait()
+    for c in kept:
+        c.wait()
 
 
 def scratch():
@@ -163,33 +179,34 @@
 
 VMEM_SPEC = pl.BlockSpec(memory_space=pltpu.VMEM)
 ANY_SPEC = pl.BlockSpec(memory_space=pl.ANY)
+HBM_SPEC = pl.BlockSpec(memory_space=pltpu.HBM)
+CUTS = 4
 SMEM_SPEC = pl.BlockSpec(memory_space=pltpu.SMEM)
 
 
 def near_spectra(offsets, blocks, forward):
+    spread = (np.arange(HALF)[:, None] // FB == np.arange(HALF)[None, :]).astype(jnp.bfloat16)
     return pl.pallas_call(
         near_kernel,
-        out_shape=jax.ShapeDtypeStruct((BLOCKS, 2, PAIRS, 2 * FB, HALF), BF16),
-        in_specs=[SMEM_SPEC] + [ANY_SPEC] * 8 + [VMEM_SPEC],
-        out_specs=VMEM_SPEC,
-        scratch_shapes=scratch() + [pltpu.SemaphoreType.DMA((8,))],
-        compiler_params=pltpu.CompilerParams(vmem_limit_bytes=16 * 1024 * 1024),
+        out_shape=[
+            jax.ShapeDtypeStruct((BLOCKS, 2, PAIRS, 2 * FB, HALF), BF16),
+            jax.ShapeDtypeStruct((BLOCKS, HALF, SECT), BF16),
+            jax.ShapeDtypeStruct((8, 128), F32),
+        ],
+        in_specs=[SMEM_SPEC] + [ANY_SPEC] * 8 + [VMEM_SPEC] * 2,
+        out_specs=[HBM_SPEC, HBM_SPEC, VMEM_SPEC],
+        scratch_shapes=[
+            pltpu.VMEM((BLOCKS, 2, PAIRS, 2 * FB, HALF), BF16),
+            pltpu.VMEM((BLOCKS, HALF, SECT), BF16),
+        ] + scratch() + [
+            pltpu.SemaphoreType.DMA((8,)),
+            pltpu.SemaphoreType.DMA((PAIRS,)),
+            pltpu.SemaphoreType.DMA((CUTS,)),
+        ],
+        compiler_params=pltpu.CompilerParams(vmem_limit_bytes=58 * 1024 * 1024),
         cost_estimate=pl.CostEstimate(flops=5_000_000_000, bytes_accessed=7_000_000, transcendentals=0),
         name="near_spectra",
-    )(offsets, *blocks, forward)
-
-
-def own_operand(white):
-    spread = (np.arange(HALF)[:, None] // FB == np.arange(HALF)[None, :]).astype(jnp.bfloat16)
-    return pl.pallas_call(
-        own_kernel,
-        out_shape=jax.ShapeDtypeStruct((BLOCKS, HALF, SECT), BF16),
-        in_specs=[VMEM_SPEC] * 2,
-        out_specs=VMEM_SPEC,
-        compiler_params=pltpu.CompilerParams(vmem_limit_bytes=16 * 1024 * 1024),
-        cost_estimate=pl.CostEstimate(flops=4_000_000_000, bytes_accessed=9_000_000, transcendentals=0),
-        name="own_operand",
-    )(white, jnp.asarray(spread))
+    )(offsets, *blocks, forward, jnp.asarray(spread))
 
 
 GROUP = 4
@@ -198,7 +215,7 @@
 def second_kernel(places, offsets, *refs):
     n = len(places)
     blocks, refs = refs[:n], refs[n:]
-    (white_hbm, own_hbm, forward, inverse, picks, out_hbm, series, piece, part, full, white, own,
+    (_, white_hbm, own_hbm, forward, inverse, picks, out_hbm, series, piece, part, full, white, own,
      grams, chosen, result, sem, near_sem, own_sem, out_sem) = refs
     copies = []
     core = offsets[SEGS]
@@ -230,7 +247,7 @@
                 grams[k, ri, b] = jnp.concatenate([low[ri, k], high[ri, k]], axis=0).astype(BF16)
         return carry
 
-    lax.fori_loop(0, BLOCKS // 2, pair_of_blocks, 0, unroll=8)
+    lax.fori_loop(0, BLOCKS // 2, pair_of_blocks, 0, unroll=16)
     outs = [
         pltpu.make_async_copy(
             result.at[pl.ds(g * GROUP, GROUP)], out_hbm.at[pl.ds(g * GROUP, GROUP)], out_sem.at[g]
@@ -248,12 +265,12 @@
         o.wait()
 
 
-def second_half(offsets, blocks, places, white, own, forward, inverse, picks):
+def second_half(offsets, blocks, places, token, white, own, forward, inverse, picks):
     n = len(blocks)
     return pl.pallas_call(
         functools.partial(second_kernel, places),
         out_shape=jax.ShapeDtypeStruct((OWN, NPART, NLAG), F32),
-        in_specs=[SMEM_SPEC] + [ANY_SPEC] * (n + 2) + [VMEM_SPEC] * 3,
+        in_specs=[SMEM_SPEC] + [ANY_SPEC] * (n + 1) + [HBM_SPEC] * 2 + [VMEM_SPEC] * 3,
         out_specs=ANY_SPEC,
         scratch_shapes=scratch() + [
             pltpu.VMEM((BLOCKS, 2, PAIRS, 2 * FB, SECT), BF16),
@@ -266,10 +283,10 @@
             pltpu.SemaphoreType.DMA,
             pltpu.SemaphoreType.DMA((OWN // GROUP,)),
         ],
-        compiler_params=pltpu.CompilerParams(vmem_limit_bytes=34 * 1024 * 1024),
+        compiler_params=pltpu.CompilerParams(vmem_limit_bytes=58 * 1024 * 1024),
         cost_estimate=pl.CostEstimate(flops=8_000_000_000, bytes_accessed=20_000_000, transcendentals=0),
         name="far_and_cross",
-    )(offsets, *blocks, white, own, forward, inverse, picks)
+    )(offsets, *blocks, token, white, own, forward, inverse, picks)
 
 
 def per_device(record, partners, offsets):
@@ -285,6 +302,7 @@
     )
 
     onward = [(i, (i + 2 - 4 * (i % 2)) % 16) for i in range(16)]
+    further = [(i, (i + 4 - 8 * (i % 2)) % 16) for i in range(16)]
     across = [(i, i ^ 1) for i in range(16)]
 
     def send(v, pairs):
@@ -293,23 +311,19 @@
     def half(v):
         return lax.dynamic_slice_in_dim(v, core * 8, 8, 0)
 
-    tie = lax.optimization_barrier
     other = send(mine, across)
     m1, o1 = send(mine, onward), send(other, onward)
     m2, o2 = send(m1, onward), send(o1, onward)
     xm1, xo1 = send(m1, across), send(o1, across)
     m3, o3 = send(m2, onward), send(o2, onward)
+    m4, o4 = send(half(m2), further), send(half(o2), further)
     xm2, xo2 = send(m2, across), send(o2, across)
     near = [mine, other, m1, o1, xm1, xo1, m2, o2]
     numbers = jnp.concatenate([offsets, core[None]])
-    white = near_spectra(numbers, near, forward)
-    m3, o3, white = tie((m3, o3, white))
-    m4, o4 = send(half(m3), onward), send(half(o3), onward)
+    white, own, token = near_spectra(numbers, near, forward)
+    m3, o3, m4, o4, token = lax.optimization_barrier((m3, o3, m4, o4, token))
     xm3, xo3 = send(m3, across), send(o3, across)
-    own = own_operand(white)
-    m4, o4, own = tie((m4, o4, own))
     xm4, xo4 = send(m4, across), send(o4, across)
-
     far = [xm2, xo2, m3, o3, xm3, xo3, m4, xo4, o4, xm4]
     places = [(i, 0) for i in range(6)] + [(6, 1), (6, 2), (7, 1), (7, 2)]
 
@@ -319,7 +333,7 @@
     origin = ((place + toward * steps) % 16) ^ swap
     channel = jnp.repeat(origin * OWN, OWN) + np.tile(np.arange(OWN, dtype=np.int32), 16)
     picks = ((partners % SECT)[:, :, None] == channel).astype(BF16)
-    return second_half(numbers, far, places, white, own, forward, inverse, picks)
+    return second_half(numbers, far, places, token, white, own, forward, inverse, picks)
 
 
 def solution(mesh):

time: 76.8 us -> 75.4 us (0.982)
  Pallas kernels: 22.9 us -> 28.2 us
  waiting for transfers between devices: 7.04 us -> 2.29 us
  local copies, waits for them, and re-layouts: 5.17 us -> 1.88 us
  other arithmetic: 0.37 us -> 1.77 us
    ppermute x17, waiting for transfers between devices: 7.04 us -> 2.29 us  [send(): return lax.ppermute(v, 'pair', pairs)]
    pallas_call x2 -> x1, Pallas kernels: 7.99 us -> 11.8 us  [near_spectra(): pl.pallas_call(near_kernel, out_shape=[jax.ShapeDtypeStruct((BLOCKS, 2, P...]
    unnamed x24 -> x48, local copies, waits for them, and re-layouts: 5.07 us -> 1.78 us
    pallas_call x1, Pallas kernels: 14.9 us -> 16.4 us  [second_half(): pl.pallas_call(functools.partial(second_kernel, places), out_shape=jax.Sh...]
    convert_element_type x1, other arithmetic: 0.2 us -> 1.04 us  [per_device(): picks = ((partners % SECT)[:, :, None] == channel).astype(BF16)]
  transfers between devices with their start and end apart: 17 -> 17, of which waited for: 6 -> 2; matrix products, arithmetic and copies ran while one was open for 1% -> 2% of each run, Pallas kernels for 10% -> 16%
where the time goes in v2:
time: 75.4 us; the launch traced here: 75.2 us
  Pallas kernels  28.2 us (37%)
  starting transfers between devices  24.4 us (32%)
  blocking collectives  14.9 us (20%)
  waiting for transfers between devices  2.29 us (3%)
  local copies, waits for them, and re-layouts  1.88 us (2%)
  other arithmetic  1.77 us (2%)
  matrix products  1.33 us (2%)
    ppermute x17, starting transfers between devices, send(): return lax.ppermute(v, 'pair', pairs)  24.4 us
    pallas_call x1, Pallas kernels, second_half(): pl.pallas_call(functools.partial(second_kernel, places), out_shape=jax.Sh...  16.4 us
    all_to_all x1, blocking collectives, per_device(): lax.all_to_all(rows.reshape(SHARDS, OWN, SHARD), 'tm', split_axis=0, conc...  14.9 us
    pallas_call x1, Pallas kernels, near_spectra(): pl.pallas_call(near_kernel, out_shape=[jax.ShapeDtypeStruct((BLOCKS, 2, P...  11.8 us
    ppermute x17, waiting for transfers between devices, send(): return lax.ppermute(v, 'pair', pairs)  2.29 us
    unnamed x48, local copies, waits for them, and re-layouts  1.78 us
  transfers between devices with their start and end apart: 17, of which 2 were waited for; matrix products, arithmetic and copies ran while one was open for 2% of the time, Pallas kernels for 16%

profile of v2, /device:TPU:1, one launch (start us, length us, event | category | flops | bytes accessed | tf_op | source)
XLA Modules:
  0.0 75.2 jit_solution(3021286712541521405)
XLA Ops:
  0.0 0.0 copy-start.5
  0.0 0.9 %copy-done = bf16[512,16,16]{0,2,1:T(8,128)(2,1)S(1)} copy-done((bf16[512,16,16]{0,2,1:T(8,128)(2,1)S(1)}, bf16[512,16,16]{0,2,1:T(8,128)(2,1)}, u32[]{:S(2)}) %copy-start) | copy-done | bytes 262168
  1.0 1.3 %convolution_bitcast_fusion = bf16[16,16,512]{2,1,0:T(8,128)(2,1)S(1)} fusion(bf16[512,512,1]{1,0,2:T(8,128)(2,1)} %constant.75, bf16[512,16,16]{0,2,1:T(8,128)(2,1)S(1)} %copy-done), kind=kOutput, calls=%fused_computation | convolution fusion | flops 134217728 | bytes 1048576 | tf_op jit(solution)/shard_map/dot_general | solution.py:299
  2.3 14.9 %all_to_all.5.refs_0_ = bf16[16,16,512]{2,1,0:T(8,128)(2,1)S(1)} all-to-all(bf16[16,16,512]{2,1,0:T(8,128)(2,1)S(1)} %convolution_bitcast_fusion), channel_id=1, replica_groups=mesh['tm'=16,'pair'=16] {'tm'}, dimensions={0} | all-to-all | bytes 524288 | tf_op jit(solution)/shard_map/all_to_all | solution.py:300
  17.2 2.1 %collective-permute-start.3 = (bf16[16,16,512]{2,1,0:T(8,128)(2,1)S(1)}, bf16[16,16,512]{2,1,0:T(8,128)(2,1)S(1)}, u32[]{:S(2)}, u32[]{:S(2)}) collective-permute-start(bf16[16,16,512]{2,1,0:T(8,128)(2,1)S(1)} %all_to_all.5.refs_0_), channel_id=1, source_target_pairs={{0,1},{1,0},{2,3},{3,2},{4,5},{5,4},{6,7},{7,6},{8,9},{9,8},{10,11... | collective-permute-start | bytes 786440 | tf_op jit(solution)/shard_map/ppermute | solution.py:309
  19.3 5.6 %collective-permute-start = (bf16[16,16,512]{2,1,0:T(8,128)(2,1)S(1)}, bf16[16,16,512]{2,1,0:T(8,128)(2,1)S(1)}, u32[]{:S(2)}, u32[]{:S(2)}) collective-permute-start(bf16[16,16,512]{2,1,0:T(8,128)(2,1)S(1)} %all_to_all.5.refs_0_), channel_id=1, source_target_pairs={{0,2},{1,15},{2,4},{3,1},{4,6},{5,3},{6,8},{7,5},{8,10},{9,7},{10,... | collective-permute-start | bytes 786440 | tf_op jit(solution)/shard_map/ppermute | solution.py:309
  24.9 0.0 collective-permute-done.3.refs_1_
  24.9 1.2 %collective-permute-start.4 = (bf16[16,16,512]{2,1,0:T(8,128)(2,1)S(1)}, bf16[16,16,512]{2,1,0:T(8,128)(2,1)S(1)}, u32[]{:S(2)}, u32[]{:S(2)}) collective-permute-start(bf16[16,16,512]{2,1,0:T(8,128)(2,1)S(1)} %collective-permute-done.3.refs_1_), channel_id=1, source_target_pairs={{0,2},{1,15},{2,4},{3,1},{4,6},{5,3},{6,8},{7,5},{8,10},{9,7},{10,... | collective-permute-start | bytes 786440 | tf_op jit(solution)/shard_map/ppermute | solution.py:309
  26.1 2.1 %collective-permute-done.refs_2_ = bf16[16,16,512]{2,1,0:T(8,128)(2,1)S(1)} collective-permute-done((bf16[16,16,512]{2,1,0:T(8,128)(2,1)S(1)}, bf16[16,16,512]{2,1,0:T(8,128)(2,1)S(1)}, u32[]{:S(2)}, u32[]{:S(2)}) %collective-permute-start) | collective-permute-done | bytes 262176 | tf_op jit(solution)/shard_map/ppermute | solution.py:309
  28.2 3.1 %collective-permute-start.1 = (bf16[16,16,512]{2,1,0:T(8,128)(2,1)S(1)}, bf16[16,16,512]{2,1,0:T(8,128)(2,1)S(1)}, u32[]{:S(2)}, u32[]{:S(2)}) collective-permute-start(bf16[16,16,512]{2,1,0:T(8,128)(2,1)S(1)} %collective-permute-done.refs_2_), channel_id=1, source_target_pairs={{0,2},{1,15},{2,4},{3,1},{4,6},{5,3},{6,8},{7,5},{8,10},{9,7},{10,... | collective-permute-start | bytes 786440 | tf_op jit(solution)/shard_map/ppermute | solution.py:309
  31.3 0.0 collective-permute-done.4.refs_3_
  31.3 2.8 %collective-permute-start.5 = (bf16[16,16,512]{2,1,0:T(8,128)(2,1)S(1)}, bf16[16,16,512]{2,1,0:T(8,128)(2,1)S(1)}, u32[]{:S(2)}, u32[]{:S(2)}) collective-permute-start(bf16[16,16,512]{2,1,0:T(8,128)(2,1)S(1)} %collective-permute-done.4.refs_3_), channel_id=1, source_target_pairs={{0,2},{1,15},{2,4},{3,1},{4,6},{5,3},{6,8},{7,5},{8,10},{9,7},{10,... | collective-permute-start | bytes 786440 | tf_op jit(solution)/shard_map/ppermute | solution.py:309
  34.2 0.1 broadcast_add_fusion
  34.2 0.0 collective-permute-start.11
  34.3 0.5 collective-permute-start.12
  34.8 0.6 pad_add_fusion.offsets
  35.4 0.0 collective-permute-done.1.refs_6_
  35.4 1.2 %collective-permute-start.9 = (bf16[8,16,512]{2,1,0:T(8,128)(2,1)S(1)}, bf16[8,16,512]{2,1,0:T(8,128)(2,1)S(1)}, u32[]{:S(2)}, u32[]{:S(2)}) collective-permute-start(bf16[8,16,512]{2,1,0:T(8,128)(2,1)S(1)} %constant_dynamic-slice_fusion.1), channel_id=1, source_target_pairs={{0,4},{1,13},{2,6},{3,15},{4,8},{5,1},{6,10},{7,3},{8,12},{9,5},{1... | collective-permute-start | bytes 393224 | tf_op jit(solution)/shard_map/ppermute | solution.py:309
  36.7 1.3 %collective-permute-start.7 = (bf16[16,16,512]{2,1,0:T(8,128)(2,1)S(1)}, bf16[16,16,512]{2,1,0:T(8,128)(2,1)S(1)}, u32[]{:S(2)}, u32[]{:S(2)}) collective-permute-start(bf16[16,16,512]{2,1,0:T(8,128)(2,1)S(1)} %collective-permute-done.1.refs_6_), channel_id=1, source_target_pairs={{0,2},{1,15},{2,4},{3,1},{4,6},{5,3},{6,8},{7,5},{8,10},{9,7},{10,... | collective-permute-start | bytes 786440 | tf_op jit(solution)/shard_map/ppermute | solution.py:309
  38.0 2.0 %collective-permute-start.2 = (bf16[16,16,512]{2,1,0:T(8,128)(2,1)S(1)}, bf16[16,16,512]{2,1,0:T(8,128)(2,1)S(1)}, u32[]{:S(2)}, u32[]{:S(2)}) collective-permute-start(bf16[16,16,512]{2,1,0:T(8,128)(2,1)S(1)} %collective-permute-done.1.refs_6_), channel_id=1, source_target_pairs={{0,1},{1,0},{2,3},{3,2},{4,5},{5,4},{6,7},{7,6},{8,9},{9,8},{10,11... | collective-permute-start | bytes 786440 | tf_op jit(solution)/shard_map/ppermute | solution.py:309
  39.9 0.0 copy-start.4
  40.0 0.0 collective-permute-done.11.refs_4_
  40.0 1.3 %collective-permute-start.10 = (bf16[8,16,512]{2,1,0:T(8,128)(2,1)S(1)}, bf16[8,16,512]{2,1,0:T(8,128)(2,1)S(1)}, u32[]{:S(2)}, u32[]{:S(2)}) collective-permute-start(bf16[8,16,512]{2,1,0:T(8,128)(2,1)S(1)} %constant_dynamic-slice_fusion), channel_id=1, source_target_pairs={{0,4},{1,13},{2,6},{3,15},{4,8},{5,1},{6,10},{7,3},{8,12},{9,5},{1... | collective-permute-start | bytes 393224 | tf_op jit(solution)/shard_map/ppermute | solution.py:309
  41.3 0.0 collective-permute-done.12.refs_5_
  41.3 1.7 %collective-permute-start.8 = (bf16[16,16,512]{2,1,0:T(8,128)(2,1)S(1)}, bf16[16,16,512]{2,1,0:T(8,128)(2,1)S(1)}, u32[]{:S(2)}, u32[]{:S(2)}) collective-permute-start(bf16[16,16,512]{2,1,0:T(8,128)(2,1)S(1)} %collective-permute-done.5.refs_7_), channel_id=1, source_target_pairs={{0,2},{1,15},{2,4},{3,1},{4,6},{5,3},{6,8},{7,5},{8,10},{9,7},{10,... | collective-permute-start | bytes 786440 | tf_op jit(solution)/shard_map/ppermute | solution.py:309
  43.0 11.8 %near_spectra.1 = (bf16[64,2,8,16,128]{4,3,2,1,0:T(8,128)(2,1)}, bf16[64,128,256]{2,1,0:T(8,128)(2,1)}, f32[8,128]{1,0:T(8,128)}) custom-call(s32[16]{0:T(128)} %pad_add_fusion.offsets, bf16[16,16,512]{2,1,0:T(8,128)(2,1)} %copy-done.1, bf16[16,16,512]{2,1,0:T(8,128)(2,1)} %copy-done.8, bf16[16,16,512]{2,1,0:T(8,128)(2,1)} %copy-done.9, ...), custom_call_target="tpu_custom_call" | custom-call | flops 5000000000 | bytes 7000000 | tf_op jit(solution)/shard_map/near_spectra/pallas_call | solution.py:189
  54.8 0.0 collective-permute-done.9.refs_6_
  54.8 0.5 collective-permute-start.6
  55.3 0.0 collective-permute-done.7.refs_2_
  55.3 0.0 collective-permute-done.10.refs_8_
  55.3 0.2 collective-permute-start.13
  55.5 0.4 collective-permute-start.14
  55.9 0.1 reshape.11
  56.0 0.2 collective-permute-start.16
  56.1 0.0 collective-permute-done.2.refs_0_
  56.2 0.4 collective-permute-start.15
  56.5 1.0 %compare_convert_fusion.refs_15_ = bf16[16,64,256]{2,1,0:T(8,128)(2,1)} fusion(s32[256]{0:T(256)S(1)} %reshape.11, s32[16,64]{1,0:T(8,128)S(1)} %add_select_fusion), kind=kLoop, calls=%fused_computation.1 | loop fusion | flops 524288 | bytes 529408 | tf_op jit(solution)/shard_map/convert_element_type | solution.py:335
  57.6 0.0 collective-permute-done.6.refs_1_
  57.6 0.0 collective-permute-done.16.refs_9_
  57.6 0.1 collective-permute-done.15.refs_7_
  57.7 0.0 collective-permute-done.13.refs_4_
  57.7 0.0 collective-permute-done.14.refs_5_
  57.8 0.5 copy-done.14
  58.3 0.0 copy-done.21
  58.3 0.1 copy-done.22
  58.4 0.1 copy-done.17
  58.5 0.1 copy-done.18
  58.6 16.4 %far_and_cross.1 = f32[16,64,512]{2,1,0:T(8,128)} custom-call(s32[16]{0:T(128)} %pad_add_fusion.offsets, bf16[16,16,512]{2,1,0:T(8,128)(2,1)} %copy-done.12, bf16[16,16,512]{2,1,0:T(8,128)(2,1)} %copy-done.14, bf16[16,16,512]{2,1,0:T(8,128)(2,1)} %copy-done.11, bf16[16,16,512]{2,1,0:T(8,128)(2,1)} %copy-done.13, bf16[16,16,512]{2,1,0:T(8,128)(2,1)} %copy-done.17, ...), custom_call_target="tpu_custom_call" | custom-call | flops 8000000000 | bytes 20000000 | tf_op jit(solution)/shard_map/far_and_cross/pallas_call | solution.py:270
  (46 shorter events, 0.1 us)
Async XLA Ops:
  0.0 1.0 %copy-start = (bf16[512,16,16]{0,2,1:T(8,128)(2,1)S(1)}, bf16[512,16,16]{0,2,1:T(8,128)(2,1)}, u32[]{:S(2)}) copy-start(bf16[512,16,16]{0,2,1:T(8,128)(2,1)} %param.10) | copy-start | bytes 786436
  0.0 26.1 %copy-start.6 = (s32[16]{0:T(128)S(1)}, s32[16]{0:T(128)}, u32[]{:S(2)}) copy-start(s32[16]{0:T(128)} %constant.71.clone) | copy-start | bytes 196
  0.0 26.1 %copy-start.7 = (s32[16]{0:T(128)S(1)}, s32[16]{0:T(128)}, u32[]{:S(2)}) copy-start(s32[16]{0:T(128)} %constant.70.clone) | copy-start | bytes 196
  0.0 34.1 %copy-start.5 = (s32[16,16]{1,0:T(8,128)S(1)}, s32[16,16]{1,0:T(8,128)}, u32[]{:S(2)}) copy-start(s32[16,16]{1,0:T(8,128)} %constant.74) | copy-start | bytes 3076
  0.0 34.7 %copy-start.23 = (s32[15]{0:T(128)S(1)}, s32[15]{0:T(128)}, u32[]{:S(2)}) copy-start(s32[15]{0:T(128)} %param.12) | copy-start | bytes 184
  17.2 25.7 %copy-start.1 = (bf16[16,16,512]{2,1,0:T(8,128)(2,1)}, bf16[16,16,512]{2,1,0:T(8,128)(2,1)S(1)}, u32[]{:S(2)}) copy-start(bf16[16,16,512]{2,1,0:T(8,128)(2,1)S(1)} %all_to_all.5.refs_0_) | copy-start | bytes 786436
  17.2 7.7 %collective-permute-start.3 = (bf16[16,16,512]{2,1,0:T(8,128)(2,1)S(1)}, bf16[16,16,512]{2,1,0:T(8,128)(2,1)S(1)}, u32[]{:S(2)}, u32[]{:S(2)}) collective-permute-start(bf16[16,16,512]{2,1,0:T(8,128)(2,1)S(1)} %all_to_all.5.refs_0_), channel_id=1, source_target_pairs={{0,1},{1,0},{2,3},{3,2},{4,5},{5,4},{6,7},{7,6},{8,9},{9,8},{10,11... | collective-permute-start | bytes 786440 | tf_op jit(solution)/shard_map/ppermute | solution.py:309
  19.3 8.9 %collective-permute-start = (bf16[16,16,512]{2,1,0:T(8,128)(2,1)S(1)}, bf16[16,16,512]{2,1,0:T(8,128)(2,1)S(1)}, u32[]{:S(2)}, u32[]{:S(2)}) collective-permute-start(bf16[16,16,512]{2,1,0:T(8,128)(2,1)S(1)} %all_to_all.5.refs_0_), channel_id=1, source_target_pairs={{0,2},{1,15},{2,4},{3,1},{4,6},{5,3},{6,8},{7,5},{8,10},{9,7},{10,... | collective-permute-start | bytes 786440 | tf_op jit(solution)/shard_map/ppermute | solution.py:309
  24.9 18.1 %copy-start.8 = (bf16[16,16,512]{2,1,0:T(8,128)(2,1)}, bf16[16,16,512]{2,1,0:T(8,128)(2,1)S(1)}, u32[]{:S(2)}) copy-start(bf16[16,16,512]{2,1,0:T(8,128)(2,1)S(1)} %collective-permute-done.3.refs_1_) | copy-start | bytes 786436
  24.9 6.4 %collective-permute-start.4 = (bf16[16,16,512]{2,1,0:T(8,128)(2,1)S(1)}, bf16[16,16,512]{2,1,0:T(8,128)(2,1)S(1)}, u32[]{:S(2)}, u32[]{:S(2)}) collective-permute-start(bf16[16,16,512]{2,1,0:T(8,128)(2,1)S(1)} %collective-permute-done.3.refs_1_), channel_id=1, source_target_pairs={{0,2},{1,15},{2,4},{3,1},{4,6},{5,3},{6,8},{7,5},{8,10},{9,7},{10,... | collective-permute-start | bytes 786440 | tf_op jit(solution)/shard_map/ppermute | solution.py:309
  28.2 14.7 %copy-start.9 = (bf16[16,16,512]{2,1,0:T(8,128)(2,1)}, bf16[16,16,512]{2,1,0:T(8,128)(2,1)S(1)}, u32[]{:S(2)}) copy-start(bf16[16,16,512]{2,1,0:T(8,128)(2,1)S(1)} %collective-permute-done.refs_2_) | copy-start | bytes 786436
  28.2 7.2 %collective-permute-start.1 = (bf16[16,16,512]{2,1,0:T(8,128)(2,1)S(1)}, bf16[16,16,512]{2,1,0:T(8,128)(2,1)S(1)}, u32[]{:S(2)}, u32[]{:S(2)}) collective-permute-start(bf16[16,16,512]{2,1,0:T(8,128)(2,1)S(1)} %collective-permute-done.refs_2_), channel_id=1, source_target_pairs={{0,2},{1,15},{2,4},{3,1},{4,6},{5,3},{6,8},{7,5},{8,10},{9,7},{10,... | collective-permute-start | bytes 786440 | tf_op jit(solution)/shard_map/ppermute | solution.py:309
  31.3 11.6 %copy-start.10 = (bf16[16,16,512]{2,1,0:T(8,128)(2,1)}, bf16[16,16,512]{2,1,0:T(8,128)(2,1)S(1)}, u32[]{:S(2)}) copy-start(bf16[16,16,512]{2,1,0:T(8,128)(2,1)S(1)} %collective-permute-done.4.refs_3_) | copy-start | bytes 786436
  31.3 6.6 %collective-permute-start.5 = (bf16[16,16,512]{2,1,0:T(8,128)(2,1)S(1)}, bf16[16,16,512]{2,1,0:T(8,128)(2,1)S(1)}, u32[]{:S(2)}, u32[]{:S(2)}) collective-permute-start(bf16[16,16,512]{2,1,0:T(8,128)(2,1)S(1)} %collective-permute-done.4.refs_3_), channel_id=1, source_target_pairs={{0,2},{1,15},{2,4},{3,1},{4,6},{5,3},{6,8},{7,5},{8,10},{9,7},{10,... | collective-permute-start | bytes 786440 | tf_op jit(solution)/shard_map/ppermute | solution.py:309
  34.2 5.7 %collective-permute-start.11 = (bf16[16,16,512]{2,1,0:T(8,128)(2,1)S(1)}, bf16[16,16,512]{2,1,0:T(8,128)(2,1)S(1)}, u32[]{:S(2)}, u32[]{:S(2)}) collective-permute-start(bf16[16,16,512]{2,1,0:T(8,128)(2,1)S(1)} %collective-permute-done.refs_2_), channel_id=1, source_target_pairs={{0,1},{1,0},{2,3},{3,2},{4,5},{5,4},{6,7},{7,6},{8,9},{9,8},{10,11... | collective-permute-start | bytes 786440 | tf_op jit(solution)/shard_map/ppermute | solution.py:309
  34.3 7.0 %collective-permute-start.12 = (bf16[16,16,512]{2,1,0:T(8,128)(2,1)S(1)}, bf16[16,16,512]{2,1,0:T(8,128)(2,1)S(1)}, u32[]{:S(2)}, u32[]{:S(2)}) collective-permute-start(bf16[16,16,512]{2,1,0:T(8,128)(2,1)S(1)} %collective-permute-done.4.refs_3_), channel_id=1, source_target_pairs={{0,1},{1,0},{2,3},{3,2},{4,5},{5,4},{6,7},{7,6},{8,9},{9,8},{10,11... | collective-permute-start | bytes 786440 | tf_op jit(solution)/shard_map/ppermute | solution.py:309
  35.4 7.6 %copy-start.3 = (bf16[16,16,512]{2,1,0:T(8,128)(2,1)}, bf16[16,16,512]{2,1,0:T(8,128)(2,1)S(1)}, u32[]{:S(2)}) copy-start(bf16[16,16,512]{2,1,0:T(8,128)(2,1)S(1)} %collective-permute-done.1.refs_6_) | copy-start | bytes 786436
  35.4 19.3 %collective-permute-start.9 = (bf16[8,16,512]{2,1,0:T(8,128)(2,1)S(1)}, bf16[8,16,512]{2,1,0:T(8,128)(2,1)S(1)}, u32[]{:S(2)}, u32[]{:S(2)}) collective-permute-start(bf16[8,16,512]{2,1,0:T(8,128)(2,1)S(1)} %constant_dynamic-slice_fusion.1), channel_id=1, source_target_pairs={{0,4},{1,13},{2,6},{3,15},{4,8},{5,1},{6,10},{7,3},{8,12},{9,5},{1... | collective-permute-start | bytes 393224 | tf_op jit(solution)/shard_map/ppermute | solution.py:309
  36.7 18.6 %collective-permute-start.7 = (bf16[16,16,512]{2,1,0:T(8,128)(2,1)S(1)}, bf16[16,16,512]{2,1,0:T(8,128)(2,1)S(1)}, u32[]{:S(2)}, u32[]{:S(2)}) collective-permute-start(bf16[16,16,512]{2,1,0:T(8,128)(2,1)S(1)} %collective-permute-done.1.refs_6_), channel_id=1, source_target_pairs={{0,2},{1,15},{2,4},{3,1},{4,6},{5,3},{6,8},{7,5},{8,10},{9,7},{10,... | collective-permute-start | bytes 786440 | tf_op jit(solution)/shard_map/ppermute | solution.py:309
  38.0 5.0 %copy-start.2 = (bf16[16,16,512]{2,1,0:T(8,128)(2,1)}, bf16[16,16,512]{2,1,0:T(8,128)(2,1)S(1)}, u32[]{:S(2)}) copy-start(bf16[16,16,512]{2,1,0:T(8,128)(2,1)S(1)} %collective-permute-done.5.refs_7_) | copy-start | bytes 786436
  38.0 18.2 %collective-permute-start.2 = (bf16[16,16,512]{2,1,0:T(8,128)(2,1)S(1)}, bf16[16,16,512]{2,1,0:T(8,128)(2,1)S(1)}, u32[]{:S(2)}, u32[]{:S(2)}) collective-permute-start(bf16[16,16,512]{2,1,0:T(8,128)(2,1)S(1)} %collective-permute-done.1.refs_6_), channel_id=1, source_target_pairs={{0,1},{1,0},{2,3},{3,2},{4,5},{5,4},{6,7},{7,6},{8,9},{9,8},{10,11... | collective-permute-start | bytes 786440 | tf_op jit(solution)/shard_map/ppermute | solution.py:309
  39.9 16.0 %copy-start.4 = (s32[16,64]{1,0:T(8,128)S(1)}, s32[16,64]{1,0:T(8,128)}, u32[]{:S(2)}) copy-start(s32[16,64]{1,0:T(8,128)} %param.11) | copy-start | bytes 12292
  40.0 3.0 %copy-start.15 = (bf16[16,16,512]{2,1,0:T(8,128)(2,1)}, bf16[16,16,512]{2,1,0:T(8,128)(2,1)S(1)}, u32[]{:S(2)}) copy-start(bf16[16,16,512]{2,1,0:T(8,128)(2,1)S(1)} %collective-permute-done.11.refs_4_) | copy-start | bytes 786436
  40.0 15.3 %collective-permute-start.10 = (bf16[8,16,512]{2,1,0:T(8,128)(2,1)S(1)}, bf16[8,16,512]{2,1,0:T(8,128)(2,1)S(1)}, u32[]{:S(2)}, u32[]{:S(2)}) collective-permute-start(bf16[8,16,512]{2,1,0:T(8,128)(2,1)S(1)} %constant_dynamic-slice_fusion), channel_id=1, source_target_pairs={{0,4},{1,13},{2,6},{3,15},{4,8},{5,1},{6,10},{7,3},{8,12},{9,5},{1... | collective-permute-start | bytes 393224 | tf_op jit(solution)/shard_map/ppermute | solution.py:309
  41.3 1.7 %copy-start.16 = (bf16[16,16,512]{2,1,0:T(8,128)(2,1)}, bf16[16,16,512]{2,1,0:T(8,128)(2,1)S(1)}, u32[]{:S(2)}) copy-start(bf16[16,16,512]{2,1,0:T(8,128)(2,1)S(1)} %collective-permute-done.12.refs_5_) | copy-start | bytes 786436
  41.3 14.0 %collective-permute-start.8 = (bf16[16,16,512]{2,1,0:T(8,128)(2,1)S(1)}, bf16[16,16,512]{2,1,0:T(8,128)(2,1)S(1)}, u32[]{:S(2)}, u32[]{:S(2)}) collective-permute-start(bf16[16,16,512]{2,1,0:T(8,128)(2,1)S(1)} %collective-permute-done.5.refs_7_), channel_id=1, source_target_pairs={{0,2},{1,15},{2,4},{3,1},{4,6},{5,3},{6,8},{7,5},{8,10},{9,7},{10,... | collective-permute-start | bytes 786440 | tf_op jit(solution)/shard_map/ppermute | solution.py:309
  54.8 3.0 %copy-start.19 = (bf16[8,16,512]{2,1,0:T(8,128)(2,1)}, bf16[8,16,512]{2,1,0:T(8,128)(2,1)S(1)}, u32[]{:S(2)}) copy-start(bf16[8,16,512]{2,1,0:T(8,128)(2,1)S(1)} %collective-permute-done.9.refs_6_) | copy-start | bytes 393220
  54.8 2.8 %collective-permute-start.6 = (bf16[16,16,512]{2,1,0:T(8,128)(2,1)}, bf16[16,16,512]{2,1,0:T(8,128)(2,1)S(1)}, u32[]{:S(2)}, u32[]{:S(2)}) collective-permute-start(bf16[16,16,512]{2,1,0:T(8,128)(2,1)} %copy-done.2), channel_id=1, source_target_pairs={{0,1},{1,0},{2,3},{3,2},{4,5},{5,4},{6,7},{7,6},{8,9},{9,8},{10,11... | collective-permute-start | bytes 786440 | tf_op jit(solution)/shard_map/ppermute | solution.py:309
  55.3 2.5 %copy-start.11 = (bf16[16,16,512]{2,1,0:T(8,128)(2,1)}, bf16[16,16,512]{2,1,0:T(8,128)(2,1)S(1)}, u32[]{:S(2)}) copy-start(bf16[16,16,512]{2,1,0:T(8,128)(2,1)S(1)} %collective-permute-done.7.refs_2_) | copy-start | bytes 786436
  55.3 2.5 %copy-start.20 = (bf16[8,16,512]{2,1,0:T(8,128)(2,1)}, bf16[8,16,512]{2,1,0:T(8,128)(2,1)S(1)}, u32[]{:S(2)}) copy-start(bf16[8,16,512]{2,1,0:T(8,128)(2,1)S(1)} %collective-permute-done.10.refs_8_) | copy-start | bytes 393220
  55.3 2.5 %copy-start.13 = (bf16[16,16,512]{2,1,0:T(8,128)(2,1)}, bf16[16,16,512]{2,1,0:T(8,128)(2,1)S(1)}, u32[]{:S(2)}) copy-start(bf16[16,16,512]{2,1,0:T(8,128)(2,1)S(1)} %collective-permute-done.8.refs_3_) | copy-start | bytes 786436
  55.3 2.4 %collective-permute-start.13 = (bf16[16,16,512]{2,1,0:T(8,128)(2,1)S(1)}, bf16[16,16,512]{2,1,0:T(8,128)(2,1)S(1)}, u32[]{:S(2)}, u32[]{:S(2)}) collective-permute-start(bf16[16,16,512]{2,1,0:T(8,128)(2,1)S(1)} %collective-permute-done.7.refs_2_), channel_id=1, source_target_pairs={{0,1},{1,0},{2,3},{3,2},{4,5},{5,4},{6,7},{7,6},{8,9},{9,8},{10,11... | collective-permute-start | bytes 786440 | tf_op jit(solution)/shard_map/ppermute | solution.py:309
  55.5 2.2 %collective-permute-start.14 = (bf16[16,16,512]{2,1,0:T(8,128)(2,1)S(1)}, bf16[16,16,512]{2,1,0:T(8,128)(2,1)S(1)}, u32[]{:S(2)}, u32[]{:S(2)}) collective-permute-start(bf16[16,16,512]{2,1,0:T(8,128)(2,1)S(1)} %collective-permute-done.8.refs_3_), channel_id=1, source_target_pairs={{0,1},{1,0},{2,3},{3,2},{4,5},{5,4},{6,7},{7,6},{8,9},{9,8},{10,11... | collective-permute-start | bytes 786440 | tf_op jit(solution)/shard_map/ppermute | solution.py:309
  56.0 1.6 %collective-permute-start.16 = (bf16[8,16,512]{2,1,0:T(8,128)(2,1)S(1)}, bf16[8,16,512]{2,1,0:T(8,128)(2,1)S(1)}, u32[]{:S(2)}, u32[]{:S(2)}) collective-permute-start(bf16[8,16,512]{2,1,0:T(8,128)(2,1)S(1)} %collective-permute-done.9.refs_6_), channel_id=1, source_target_pairs={{0,1},{1,0},{2,3},{3,2},{4,5},{5,4},{6,7},{7,6},{8,9},{9,8},{10,11... | collective-permute-start | bytes 393224 | tf_op jit(solution)/shard_map/ppermute | solution.py:309
  56.1 1.6 %copy-start.12 = (bf16[16,16,512]{2,1,0:T(8,128)(2,1)}, bf16[16,16,512]{2,1,0:T(8,128)(2,1)S(1)}, u32[]{:S(2)}) copy-start(bf16[16,16,512]{2,1,0:T(8,128)(2,1)S(1)} %collective-permute-done.2.refs_0_) | copy-start | bytes 786436
  56.2 1.6 %collective-permute-start.15 = (bf16[8,16,512]{2,1,0:T(8,128)(2,1)S(1)}, bf16[8,16,512]{2,1,0:T(8,128)(2,1)S(1)}, u32[]{:S(2)}, u32[]{:S(2)}) collective-permute-start(bf16[8,16,512]{2,1,0:T(8,128)(2,1)S(1)} %collective-permute-done.10.refs_8_), channel_id=1, source_target_pairs={{0,1},{1,0},{2,3},{3,2},{4,5},{5,4},{6,7},{7,6},{8,9},{9,8},{10,11... | collective-permute-start | bytes 393224 | tf_op jit(solution)/shard_map/ppermute | solution.py:309
  57.6 0.7 copy-start.14
  57.6 0.7 copy-start.21
  57.7 0.7 copy-start.22
  57.7 0.7 copy-start.17
  57.7 0.8 %copy-start.18 = (bf16[16,16,512]{2,1,0:T(8,128)(2,1)}, bf16[16,16,512]{2,1,0:T(8,128)(2,1)S(1)}, u32[]{:S(2)}) copy-start(bf16[16,16,512]{2,1,0:T(8,128)(2,1)S(1)} %collective-permute-done.14.refs_5_) | copy-start | bytes 786436

commit v3 on v2

--- a/solution.py
+++ b/solution.py
@@ -132,8 +132,7 @@
 
 def near_kernel(offsets, *refs):
     blocks, refs = refs[:8], refs[8:]
-    (forward, spread, white_hbm, own_hbm, token, white, own, series, piece, part, full, sem, near_sem,
-     own_sem) = refs
+    forward, _, white_hbm, token, white, series, piece, part, full, sem, near_sem = refs
     copies = [pltpu.make_async_copy(b, series.at[i], sem.at[i]) for i, b in enumerate(blocks)]
     for c in copies:
         c.start()
@@ -147,23 +146,6 @@
         offsets, series, forward, piece, part, full, white, slice(0, HALF), lambda u: kept[u].start()
     )
     token[...] = jnp.zeros((8, 128), F32)
-    row = lax.broadcasted_iota(jnp.int32, (HALF, 2 * HALF), 0)
-    column = lax.broadcasted_iota(jnp.int32, (HALF, 2 * HALF), 1)
-    mask = (row % FB == column % FB) & (column % HALF < SEGS * FB)
-
-    def rows(b, carry):
-        spreaded = dot(spread[...], white[b].reshape(2 * HALF, HALF), NT)
-        own[b] = jnp.where(mask, spreaded, 0.0).astype(BF16)
-        return carry
-
-    outs = []
-    for i in range(CUTS):
-        cut = pl.ds(i * (BLOCKS // CUTS), BLOCKS // CUTS)
-        lax.fori_loop(i * (BLOCKS // CUTS), (i + 1) * (BLOCKS // CUTS), rows, 0, unroll=8)
-        outs.append(pltpu.make_async_copy(own.at[cut], own_hbm.at[cut], own_sem.at[i]))
-        outs[-1].start()
-    for o in outs:
-        o.wait()
     for c in kept:
         c.wait()
 
@@ -180,33 +162,28 @@
 VMEM_SPEC = pl.BlockSpec(memory_space=pltpu.VMEM)
 ANY_SPEC = pl.BlockSpec(memory_space=pl.ANY)
 HBM_SPEC = pl.BlockSpec(memory_space=pltpu.HBM)
-CUTS = 4
 SMEM_SPEC = pl.BlockSpec(memory_space=pltpu.SMEM)
 
 
-def near_spectra(offsets, blocks, forward):
-    spread = (np.arange(HALF)[:, None] // FB == np.arange(HALF)[None, :]).astype(jnp.bfloat16)
+def near_spectra(offsets, blocks, forward, picks):
     return pl.pallas_call(
         near_kernel,
         out_shape=[
             jax.ShapeDtypeStruct((BLOCKS, 2, PAIRS, 2 * FB, HALF), BF16),
-            jax.ShapeDtypeStruct((BLOCKS, HALF, SECT), BF16),
             jax.ShapeDtypeStruct((8, 128), F32),
         ],
-        in_specs=[SMEM_SPEC] + [ANY_SPEC] * 8 + [VMEM_SPEC] * 2,
-        out_specs=[HBM_SPEC, HBM_SPEC, VMEM_SPEC],
+        in_specs=[SMEM_SPEC] + [ANY_SPEC] * 8 + [VMEM_SPEC, ANY_SPEC],
+        out_specs=[HBM_SPEC, VMEM_SPEC],
         scratch_shapes=[
             pltpu.VMEM((BLOCKS, 2, PAIRS, 2 * FB, HALF), BF16),
-            pltpu.VMEM((BLOCKS, HALF, SECT), BF16),
         ] + scratch() + [
             pltpu.SemaphoreType.DMA((8,)),
             pltpu.SemaphoreType.DMA((PAIRS,)),
-            pltpu.SemaphoreType.DMA((CUTS,)),
         ],
         compiler_params=pltpu.CompilerParams(vmem_limit_bytes=58 * 1024 * 1024),
         cost_estimate=pl.CostEstimate(flops=5_000_000_000, bytes_accessed=7_000_000, transcendentals=0),
         name="near_spectra",
-    )(offsets, *blocks, forward, jnp.asarray(spread))
+    )(offsets, *blocks, forward, picks)
 
 
 GROUP = 4
@@ -215,8 +192,8 @@
 def second_kernel(places, offsets, *refs):
     n = len(places)
     blocks, refs = refs[:n], refs[n:]
-    (_, white_hbm, own_hbm, forward, inverse, picks, out_hbm, series, piece, part, full, white, own,
-     grams, chosen, result, sem, near_sem, own_sem, out_sem) = refs
+    (_, white_hbm, forward, spread, inverse, picks, out_hbm, series, piece, part, full, white, own,
+     grams, chosen, result, sem, near_sem, out_sem) = refs
     copies = []
     core = offsets[SEGS]
     for i, (b, (at, part_of)) in enumerate(zip(blocks, places)):
@@ -226,13 +203,20 @@
         c.start()
     near = pltpu.make_async_copy(white_hbm, white.at[:, :, :, :, pl.ds(0, HALF)], near_sem)
     near.start()
-    mine = pltpu.make_async_copy(own_hbm, own, own_sem)
-    mine.start()
     for c in copies:
         c.wait()
     spectra(offsets, series, forward, piece, part, full, white, slice(HALF, SECT))
     near.wait()
-    mine.wait()
+    row = lax.broadcasted_iota(jnp.int32, (HALF, 2 * HALF), 0)
+    column = lax.broadcasted_iota(jnp.int32, (HALF, 2 * HALF), 1)
+    mask = (row % FB == column % FB) & (column % HALF < SEGS * FB)
+
+    def own_rows(b, carry):
+        rows = white[b, :, :, :, :HALF].reshape(2 * HALF, HALF)
+        own[b] = jnp.where(mask, dot(spread[...], rows, NT), 0.0).astype(BF16)
+        return carry
+
+    lax.fori_loop(0, BLOCKS, own_rows, 0, unroll=8)
 
     def gram(b):
         rows = own[b]
@@ -265,12 +249,13 @@
         o.wait()
 
 
-def second_half(offsets, blocks, places, token, white, own, forward, inverse, picks):
+def second_half(offsets, blocks, places, token, white, forward, inverse, picks):
+    spread = (np.arange(HALF)[:, None] // FB == np.arange(HALF)[None, :]).astype(jnp.bfloat16)
     n = len(blocks)
     return pl.pallas_call(
         functools.partial(second_kernel, places),
         out_shape=jax.ShapeDtypeStruct((OWN, NPART, NLAG), F32),
-        in_specs=[SMEM_SPEC] + [ANY_SPEC] * (n + 1) + [HBM_SPEC] * 2 + [VMEM_SPEC] * 3,
+        in_specs=[SMEM_SPEC] + [ANY_SPEC] * (n + 1) + [HBM_SPEC] + [VMEM_SPEC] * 4,
         out_specs=ANY_SPEC,
         scratch_shapes=scratch() + [
             pltpu.VMEM((BLOCKS, 2, PAIRS, 2 * FB, SECT), BF16),
@@ -280,13 +265,12 @@
             pltpu.VMEM((OWN, NPART, NLAG), F32),
             pltpu.SemaphoreType.DMA((n,)),
             pltpu.SemaphoreType.DMA,
-            pltpu.SemaphoreType.DMA,
             pltpu.SemaphoreType.DMA((OWN // GROUP,)),
         ],
         compiler_params=pltpu.CompilerParams(vmem_limit_bytes=58 * 1024 * 1024),
         cost_estimate=pl.CostEstimate(flops=8_000_000_000, bytes_accessed=20_000_000, transcendentals=0),
         name="far_and_cross",
-    )(offsets, *blocks, token, white, own, forward, inverse, picks)
+    )(offsets, *blocks, token, white, forward, jnp.asarray(spread), inverse, picks)
 
 
 def per_device(record, partners, offsets):
@@ -320,20 +304,20 @@
     xm2, xo2 = send(m2, across), send(o2, across)
     near = [mine, other, m1, o1, xm1, xo1, m2, o2]
     numbers = jnp.concatenate([offsets, core[None]])
-    white, own, token = near_spectra(numbers, near, forward)
-    m3, o3, m4, o4, token = lax.optimization_barrier((m3, o3, m4, o4, token))
-    xm3, xo3 = send(m3, across), send(o3, across)
-    xm4, xo4 = send(m4, across), send(o4, across)
-    far = [xm2, xo2, m3, o3, xm3, xo3, m4, xo4, o4, xm4]
-    places = [(i, 0) for i in range(6)] + [(6, 1), (6, 2), (7, 1), (7, 2)]
-
     toward = 2 * (2 * core - 1)
     steps = np.array([0, 0, 1, 1, -1, -1, 2, 2, -2, -2, 3, 3, -3, -3, 4, 4], np.int32)
     swap = np.array([0, 1, 0, 1, 1, 0, 0, 1, 1, 0, 0, 1, 1, 0, 0, 1], np.int32)
     origin = ((place + toward * steps) % 16) ^ swap
     channel = jnp.repeat(origin * OWN, OWN) + np.tile(np.arange(OWN, dtype=np.int32), 16)
     picks = ((partners % SECT)[:, :, None] == channel).astype(BF16)
-    return second_half(numbers, far, places, token, white, own, forward, inverse, picks)
+    white, token = near_spectra(numbers, near, forward, picks)
+    m3, o3, m4, o4, token = lax.optimization_barrier((m3, o3, m4, o4, token))
+    xm3, xo3 = send(m3, across), send(o3, across)
+    xm4, xo4 = send(m4, across), send(o4, across)
+    far = [xm2, xo2, m3, o3, xm3, xo3, m4, xo4, o4, xm4]
+    places = [(i, 0) for i in range(6)] + [(6, 1), (6, 2), (7, 1), (7, 2)]
+
+    return second_half(numbers, far, places, token, white, forward, inverse, picks)
 
 
 def solution(mesh):

time: 75.4 us -> 75.2 us (level)
  waiting for transfers between devices: 2.29 us -> 3.35 us
  starting transfers between devices: 24.4 us -> 23.5 us
    pallas_call x1, Pallas kernels: 11.8 us -> 9.04 us  [near_spectra(): pl.pallas_call(near_kernel, out_shape=[jax.ShapeDtypeStruct((BLOCKS, 2, P...]
    pallas_call x1, Pallas kernels: 16.4 us -> 18.9 us  [second_half(): pl.pallas_call(functools.partial(second_kernel, places), out_shape=jax.Sh...]
    ppermute x17, waiting for transfers between devices: 2.29 us -> 3.35 us  [send(): return lax.ppermute(v, 'pair', pairs)]
    ppermute x17, starting transfers between devices: 24.4 us -> 23.5 us  [send(): return lax.ppermute(v, 'pair', pairs)]
  transfers between devices with their start and end apart: 17 -> 17, of which waited for: 2 -> 4; matrix products, arithmetic and copies ran while one was open for 2% -> 2% of each run, Pallas kernels for 16% -> 12%
where the time goes in v3:
time: 75.2 us; the launch traced here: 75 us
  Pallas kernels  27.9 us (37%)
  starting transfers between devices  23.5 us (31%)
  blocking collectives  14.9 us (20%)
  waiting for transfers between devices  3.35 us (4%)
  local copies, waits for them, and re-layouts  1.9 us (3%)
  other arithmetic  1.71 us (2%)
  matrix products  1.35 us (2%)
    ppermute x17, starting transfers between devices, send(): return lax.ppermute(v, 'pair', pairs)  23.5 us
    pallas_call x1, Pallas kernels, second_half(): pl.pallas_call(functools.partial(second_kernel, places), out_shape=jax.Sh...  18.9 us
    all_to_all x1, blocking collectives, per_device(): lax.all_to_all(rows.reshape(SHARDS, OWN, SHARD), 'tm', split_axis=0, conc...  14.9 us
    pallas_call x1, Pallas kernels, near_spectra(): pl.pallas_call(near_kernel, out_shape=[jax.ShapeDtypeStruct((BLOCKS, 2, P...  9.04 us
    ppermute x17, waiting for transfers between devices, send(): return lax.ppermute(v, 'pair', pairs)  3.35 us
    unnamed x48, local copies, waits for them, and re-layouts  1.8 us
  transfers between devices with their start and end apart: 17, of which 4 were waited for; matrix products, arithmetic and copies ran while one was open for 2% of the time, Pallas kernels for 12%

profile of v3, /device:TPU:1, one launch (start us, length us, event | category | flops | bytes accessed | tf_op | source)
XLA Modules:
  0.0 75.0 jit_solution(4232485063197894011)
XLA Ops:
  0.0 0.0 copy-start.5
  0.0 0.9 %copy-done = bf16[512,16,16]{0,2,1:T(8,128)(2,1)S(1)} copy-done((bf16[512,16,16]{0,2,1:T(8,128)(2,1)S(1)}, bf16[512,16,16]{0,2,1:T(8,128)(2,1)}, u32[]{:S(2)}) %copy-start) | copy-done | bytes 262168
  1.0 1.4 %convolution_bitcast_fusion = bf16[16,16,512]{2,1,0:T(8,128)(2,1)S(1)} fusion(bf16[512,512,1]{1,0,2:T(8,128)(2,1)} %constant.75, bf16[512,16,16]{0,2,1:T(8,128)(2,1)S(1)} %copy-done), kind=kOutput, calls=%fused_computation | convolution fusion | flops 134217728 | bytes 1048576 | tf_op jit(solution)/shard_map/dot_general | solution.py:283
  2.3 14.9 %all_to_all.5.refs_0_ = bf16[16,16,512]{2,1,0:T(8,128)(2,1)S(1)} all-to-all(bf16[16,16,512]{2,1,0:T(8,128)(2,1)S(1)} %convolution_bitcast_fusion), channel_id=1, replica_groups=mesh['tm'=16,'pair'=16] {'tm'}, dimensions={0} | all-to-all | bytes 524288 | tf_op jit(solution)/shard_map/all_to_all | solution.py:284
  17.2 2.1 %collective-permute-start.3 = (bf16[16,16,512]{2,1,0:T(8,128)(2,1)S(1)}, bf16[16,16,512]{2,1,0:T(8,128)(2,1)S(1)}, u32[]{:S(2)}, u32[]{:S(2)}) collective-permute-start(bf16[16,16,512]{2,1,0:T(8,128)(2,1)S(1)} %all_to_all.5.refs_0_), channel_id=1, source_target_pairs={{0,1},{1,0},{2,3},{3,2},{4,5},{5,4},{6,7},{7,6},{8,9},{9,8},{10,11... | collective-permute-start | bytes 786440 | tf_op jit(solution)/shard_map/ppermute | solution.py:293
  19.4 5.7 %collective-permute-start = (bf16[16,16,512]{2,1,0:T(8,128)(2,1)S(1)}, bf16[16,16,512]{2,1,0:T(8,128)(2,1)S(1)}, u32[]{:S(2)}, u32[]{:S(2)}) collective-permute-start(bf16[16,16,512]{2,1,0:T(8,128)(2,1)S(1)} %all_to_all.5.refs_0_), channel_id=1, source_target_pairs={{0,2},{1,15},{2,4},{3,1},{4,6},{5,3},{6,8},{7,5},{8,10},{9,7},{10,... | collective-permute-start | bytes 786440 | tf_op jit(solution)/shard_map/ppermute | solution.py:293
  25.0 0.0 collective-permute-done.3.refs_1_
  25.0 1.1 %collective-permute-start.4 = (bf16[16,16,512]{2,1,0:T(8,128)(2,1)S(1)}, bf16[16,16,512]{2,1,0:T(8,128)(2,1)S(1)}, u32[]{:S(2)}, u32[]{:S(2)}) collective-permute-start(bf16[16,16,512]{2,1,0:T(8,128)(2,1)S(1)} %collective-permute-done.3.refs_1_), channel_id=1, source_target_pairs={{0,2},{1,15},{2,4},{3,1},{4,6},{5,3},{6,8},{7,5},{8,10},{9,7},{10,... | collective-permute-start | bytes 786440 | tf_op jit(solution)/shard_map/ppermute | solution.py:293
  26.1 0.1 broadcast_add_fusion
  26.2 0.1 reshape.11
  26.3 2.1 %collective-permute-done.refs_2_ = bf16[16,16,512]{2,1,0:T(8,128)(2,1)S(1)} collective-permute-done((bf16[16,16,512]{2,1,0:T(8,128)(2,1)S(1)}, bf16[16,16,512]{2,1,0:T(8,128)(2,1)S(1)}, u32[]{:S(2)}, u32[]{:S(2)}) %collective-permute-start) | collective-permute-done | bytes 262176 | tf_op jit(solution)/shard_map/ppermute | solution.py:293
  28.3 3.1 %collective-permute-start.1 = (bf16[16,16,512]{2,1,0:T(8,128)(2,1)S(1)}, bf16[16,16,512]{2,1,0:T(8,128)(2,1)S(1)}, u32[]{:S(2)}, u32[]{:S(2)}) collective-permute-start(bf16[16,16,512]{2,1,0:T(8,128)(2,1)S(1)} %collective-permute-done.refs_2_), channel_id=1, source_target_pairs={{0,2},{1,15},{2,4},{3,1},{4,6},{5,3},{6,8},{7,5},{8,10},{9,7},{10,... | collective-permute-start | bytes 786440 | tf_op jit(solution)/shard_map/ppermute | solution.py:293
  31.5 0.0 collective-permute-done.4.refs_3_
  31.5 2.8 %collective-permute-start.5 = (bf16[16,16,512]{2,1,0:T(8,128)(2,1)S(1)}, bf16[16,16,512]{2,1,0:T(8,128)(2,1)S(1)}, u32[]{:S(2)}, u32[]{:S(2)}) collective-permute-start(bf16[16,16,512]{2,1,0:T(8,128)(2,1)S(1)} %collective-permute-done.4.refs_3_), channel_id=1, source_target_pairs={{0,2},{1,15},{2,4},{3,1},{4,6},{5,3},{6,8},{7,5},{8,10},{9,7},{10,... | collective-permute-start | bytes 786440 | tf_op jit(solution)/shard_map/ppermute | solution.py:293
  34.3 1.0 %compare_convert_fusion.refs_9_.refs_15_ = bf16[16,64,256]{2,1,0:T(8,128)(2,1)} fusion(s32[256]{0:T(256)S(1)} %reshape.11, s32[16,64]{1,0:T(8,128)S(1)} %add_select_fusion), kind=kLoop, calls=%fused_computation.1 | loop fusion | flops 524288 | bytes 529408 | tf_op jit(solution)/shard_map/convert_element_type | solution.py:312
  35.3 0.0 collective-permute-start.11
  35.3 0.5 collective-permute-start.12
  35.8 0.6 pad_add_fusion.offsets
  36.4 0.0 collective-permute-done.1.refs_6_
  36.4 1.0 %collective-permute-start.9 = (bf16[8,16,512]{2,1,0:T(8,128)(2,1)S(1)}, bf16[8,16,512]{2,1,0:T(8,128)(2,1)S(1)}, u32[]{:S(2)}, u32[]{:S(2)}) collective-permute-start(bf16[8,16,512]{2,1,0:T(8,128)(2,1)S(1)} %constant_dynamic-slice_fusion.1), channel_id=1, source_target_pairs={{0,4},{1,13},{2,6},{3,15},{4,8},{5,1},{6,10},{7,3},{8,12},{9,5},{1... | collective-permute-start | bytes 393224 | tf_op jit(solution)/shard_map/ppermute | solution.py:293
  37.4 0.7 collective-permute-start.7
  38.1 0.0 collective-permute-done.5.refs_7_
  38.1 2.3 %collective-permute-start.2 = (bf16[16,16,512]{2,1,0:T(8,128)(2,1)S(1)}, bf16[16,16,512]{2,1,0:T(8,128)(2,1)S(1)}, u32[]{:S(2)}, u32[]{:S(2)}) collective-permute-start(bf16[16,16,512]{2,1,0:T(8,128)(2,1)S(1)} %collective-permute-done.1.refs_6_), channel_id=1, source_target_pairs={{0,1},{1,0},{2,3},{3,2},{4,5},{5,4},{6,7},{7,6},{8,9},{9,8},{10,11... | collective-permute-start | bytes 786440 | tf_op jit(solution)/shard_map/ppermute | solution.py:293
  40.4 0.0 collective-permute-done.11.refs_4_
  40.4 1.4 %collective-permute-start.10 = (bf16[8,16,512]{2,1,0:T(8,128)(2,1)S(1)}, bf16[8,16,512]{2,1,0:T(8,128)(2,1)S(1)}, u32[]{:S(2)}, u32[]{:S(2)}) collective-permute-start(bf16[8,16,512]{2,1,0:T(8,128)(2,1)S(1)} %constant_dynamic-slice_fusion), channel_id=1, source_target_pairs={{0,4},{1,13},{2,6},{3,15},{4,8},{5,1},{6,10},{7,3},{8,12},{9,5},{1... | collective-permute-start | bytes 393224 | tf_op jit(solution)/shard_map/ppermute | solution.py:293
  41.9 0.0 collective-permute-done.12.refs_5_
  41.9 1.2 %collective-permute-start.8 = (bf16[16,16,512]{2,1,0:T(8,128)(2,1)S(1)}, bf16[16,16,512]{2,1,0:T(8,128)(2,1)S(1)}, u32[]{:S(2)}, u32[]{:S(2)}) collective-permute-start(bf16[16,16,512]{2,1,0:T(8,128)(2,1)S(1)} %collective-permute-done.5.refs_7_), channel_id=1, source_target_pairs={{0,2},{1,15},{2,4},{3,1},{4,6},{5,3},{6,8},{7,5},{8,10},{9,7},{10,... | collective-permute-start | bytes 786440 | tf_op jit(solution)/shard_map/ppermute | solution.py:293
  43.1 9.0 %near_spectra.1 = (bf16[64,2,8,16,128]{4,3,2,1,0:T(8,128)(2,1)}, f32[8,128]{1,0:T(8,128)}) custom-call(s32[16]{0:T(128)} %pad_add_fusion.offsets, bf16[16,16,512]{2,1,0:T(8,128)(2,1)} %copy-done.1, bf16[16,16,512]{2,1,0:T(8,128)(2,1)} %copy-done.8, bf16[16,16,512]{2,1,0:T(8,128)(2,1)} %copy-done.10, bf16[16,16,512]{2,1,0:T(8,128)(2,1)} %copy-done.12, ...), custom_call_target="tpu_custom_call" | custom-call | flops 5000000000 | bytes 7000000 | tf_op jit(solution)/shard_map/near_spectra/pallas_call | solution.py:169
  52.2 0.0 collective-permute-done.9.refs_6_
  52.2 0.5 collective-permute-start.6
  52.7 0.0 collective-permute-done.7.refs_2_
  52.7 0.0 collective-permute-done.10.refs_8_
  52.7 0.0 collective-permute-done.8.refs_3_
  52.7 0.3 collective-permute-start.13
  53.0 0.3 collective-permute-start.14
  53.3 0.2 collective-permute-start.16
  53.5 0.0 collective-permute-done.2.refs_0_
  53.5 0.3 collective-permute-start.15
  53.8 0.2 collective-permute-done.6.refs_1_
  54.0 0.9 %collective-permute-done.16.refs_9_ = bf16[8,16,512]{2,1,0:T(8,128)(2,1)S(1)} collective-permute-done((bf16[8,16,512]{2,1,0:T(8,128)(2,1)S(1)}, bf16[8,16,512]{2,1,0:T(8,128)(2,1)S(1)}, u32[]{:S(2)}, u32[]{:S(2)}) %collective-permute-start.16) | collective-permute-done | bytes 131104 | tf_op jit(solution)/shard_map/ppermute | solution.py:293
  54.9 0.2 collective-permute-done.15.refs_7_
  55.1 0.0 collective-permute-done.13.refs_4_
  55.1 0.0 collective-permute-done.14.refs_5_
  55.2 0.4 copy-done.21
  55.6 0.2 copy-done.22
  55.7 0.1 copy-done.17
  55.8 0.1 copy-done.18
  56.0 18.9 %far_and_cross.1 = f32[16,64,512]{2,1,0:T(8,128)} custom-call(s32[16]{0:T(128)} %pad_add_fusion.offsets, bf16[16,16,512]{2,1,0:T(8,128)(2,1)} %copy-done.11, bf16[16,16,512]{2,1,0:T(8,128)(2,1)} %copy-done.14, bf16[16,16,512]{2,1,0:T(8,128)(2,1)} %copy-done.9, bf16[16,16,512]{2,1,0:T(8,128)(2,1)} %copy-done.13, bf16[16,16,512]{2,1,0:T(8,128)(2,1)} %copy-done.17, ...), custom_call_target="tpu_custom_call" | custom-call | flops 8000000000 | bytes 20000000 | tf_op jit(solution)/shard_map/far_and_cross/pallas_call | solution.py:255
  (46 shorter events, 0.1 us)
Async XLA Ops:
  0.0 1.0 %copy-start = (bf16[512,16,16]{0,2,1:T(8,128)(2,1)S(1)}, bf16[512,16,16]{0,2,1:T(8,128)(2,1)}, u32[]{:S(2)}) copy-start(bf16[512,16,16]{0,2,1:T(8,128)(2,1)} %param.10) | copy-start | bytes 786436
  0.0 19.3 %copy-start.6 = (s32[16]{0:T(128)S(1)}, s32[16]{0:T(128)}, u32[]{:S(2)}) copy-start(s32[16]{0:T(128)} %constant.70.clone) | copy-start | bytes 196
  0.0 19.3 %copy-start.7 = (s32[16]{0:T(128)S(1)}, s32[16]{0:T(128)}, u32[]{:S(2)}) copy-start(s32[16]{0:T(128)} %constant.69.clone) | copy-start | bytes 196
  0.0 26.1 %copy-start.5 = (s32[16,16]{1,0:T(8,128)S(1)}, s32[16,16]{1,0:T(8,128)}, u32[]{:S(2)}) copy-start(s32[16,16]{1,0:T(8,128)} %constant.74) | copy-start | bytes 3076
  0.0 26.2 %copy-start.4 = (s32[16,64]{1,0:T(8,128)S(1)}, s32[16,64]{1,0:T(8,128)}, u32[]{:S(2)}) copy-start(s32[16,64]{1,0:T(8,128)} %param.11) | copy-start | bytes 12292
  1.0 34.8 %copy-start.23 = (s32[15]{0:T(128)S(1)}, s32[15]{0:T(128)}, u32[]{:S(2)}) copy-start(s32[15]{0:T(128)} %param.12) | copy-start | bytes 184
  17.2 25.8 %copy-start.1 = (bf16[16,16,512]{2,1,0:T(8,128)(2,1)}, bf16[16,16,512]{2,1,0:T(8,128)(2,1)S(1)}, u32[]{:S(2)}) copy-start(bf16[16,16,512]{2,1,0:T(8,128)(2,1)S(1)} %all_to_all.5.refs_0_) | copy-start | bytes 786436
  17.2 7.8 %collective-permute-start.3 = (bf16[16,16,512]{2,1,0:T(8,128)(2,1)S(1)}, bf16[16,16,512]{2,1,0:T(8,128)(2,1)S(1)}, u32[]{:S(2)}, u32[]{:S(2)}) collective-permute-start(bf16[16,16,512]{2,1,0:T(8,128)(2,1)S(1)} %all_to_all.5.refs_0_), channel_id=1, source_target_pairs={{0,1},{1,0},{2,3},{3,2},{4,5},{5,4},{6,7},{7,6},{8,9},{9,8},{10,11... | collective-permute-start | bytes 786440 | tf_op jit(solution)/shard_map/ppermute | solution.py:293
  19.4 9.0 %collective-permute-start = (bf16[16,16,512]{2,1,0:T(8,128)(2,1)S(1)}, bf16[16,16,512]{2,1,0:T(8,128)(2,1)S(1)}, u32[]{:S(2)}, u32[]{:S(2)}) collective-permute-start(bf16[16,16,512]{2,1,0:T(8,128)(2,1)S(1)} %all_to_all.5.refs_0_), channel_id=1, source_target_pairs={{0,2},{1,15},{2,4},{3,1},{4,6},{5,3},{6,8},{7,5},{8,10},{9,7},{10,... | collective-permute-start | bytes 786440 | tf_op jit(solution)/shard_map/ppermute | solution.py:293
  25.0 18.1 %copy-start.8 = (bf16[16,16,512]{2,1,0:T(8,128)(2,1)}, bf16[16,16,512]{2,1,0:T(8,128)(2,1)S(1)}, u32[]{:S(2)}) copy-start(bf16[16,16,512]{2,1,0:T(8,128)(2,1)S(1)} %collective-permute-done.3.refs_1_) | copy-start | bytes 786436
  25.0 6.4 %collective-permute-start.4 = (bf16[16,16,512]{2,1,0:T(8,128)(2,1)S(1)}, bf16[16,16,512]{2,1,0:T(8,128)(2,1)S(1)}, u32[]{:S(2)}, u32[]{:S(2)}) collective-permute-start(bf16[16,16,512]{2,1,0:T(8,128)(2,1)S(1)} %collective-permute-done.3.refs_1_), channel_id=1, source_target_pairs={{0,2},{1,15},{2,4},{3,1},{4,6},{5,3},{6,8},{7,5},{8,10},{9,7},{10,... | collective-permute-start | bytes 786440 | tf_op jit(solution)/shard_map/ppermute | solution.py:293
  28.3 14.7 %copy-start.10 = (bf16[16,16,512]{2,1,0:T(8,128)(2,1)}, bf16[16,16,512]{2,1,0:T(8,128)(2,1)S(1)}, u32[]{:S(2)}) copy-start(bf16[16,16,512]{2,1,0:T(8,128)(2,1)S(1)} %collective-permute-done.refs_2_) | copy-start | bytes 786436
  28.3 8.1 %collective-permute-start.1 = (bf16[16,16,512]{2,1,0:T(8,128)(2,1)S(1)}, bf16[16,16,512]{2,1,0:T(8,128)(2,1)S(1)}, u32[]{:S(2)}, u32[]{:S(2)}) collective-permute-start(bf16[16,16,512]{2,1,0:T(8,128)(2,1)S(1)} %collective-permute-done.refs_2_), channel_id=1, source_target_pairs={{0,2},{1,15},{2,4},{3,1},{4,6},{5,3},{6,8},{7,5},{8,10},{9,7},{10,... | collective-permute-start | bytes 786440 | tf_op jit(solution)/shard_map/ppermute | solution.py:293
  31.5 11.6 %copy-start.12 = (bf16[16,16,512]{2,1,0:T(8,128)(2,1)}, bf16[16,16,512]{2,1,0:T(8,128)(2,1)S(1)}, u32[]{:S(2)}) copy-start(bf16[16,16,512]{2,1,0:T(8,128)(2,1)S(1)} %collective-permute-done.4.refs_3_) | copy-start | bytes 786436
  31.5 6.7 %collective-permute-start.5 = (bf16[16,16,512]{2,1,0:T(8,128)(2,1)S(1)}, bf16[16,16,512]{2,1,0:T(8,128)(2,1)S(1)}, u32[]{:S(2)}, u32[]{:S(2)}) collective-permute-start(bf16[16,16,512]{2,1,0:T(8,128)(2,1)S(1)} %collective-permute-done.4.refs_3_), channel_id=1, source_target_pairs={{0,2},{1,15},{2,4},{3,1},{4,6},{5,3},{6,8},{7,5},{8,10},{9,7},{10,... | collective-permute-start | bytes 786440 | tf_op jit(solution)/shard_map/ppermute | solution.py:293
  35.3 5.2 %collective-permute-start.11 = (bf16[16,16,512]{2,1,0:T(8,128)(2,1)S(1)}, bf16[16,16,512]{2,1,0:T(8,128)(2,1)S(1)}, u32[]{:S(2)}, u32[]{:S(2)}) collective-permute-start(bf16[16,16,512]{2,1,0:T(8,128)(2,1)S(1)} %collective-permute-done.refs_2_), channel_id=1, source_target_pairs={{0,1},{1,0},{2,3},{3,2},{4,5},{5,4},{6,7},{7,6},{8,9},{9,8},{10,11... | collective-permute-start | bytes 786440 | tf_op jit(solution)/shard_map/ppermute | solution.py:293
  35.3 6.6 %collective-permute-start.12 = (bf16[16,16,512]{2,1,0:T(8,128)(2,1)S(1)}, bf16[16,16,512]{2,1,0:T(8,128)(2,1)S(1)}, u32[]{:S(2)}, u32[]{:S(2)}) collective-permute-start(bf16[16,16,512]{2,1,0:T(8,128)(2,1)S(1)} %collective-permute-done.4.refs_3_), channel_id=1, source_target_pairs={{0,1},{1,0},{2,3},{3,2},{4,5},{5,4},{6,7},{7,6},{8,9},{9,8},{10,11... | collective-permute-start | bytes 786440 | tf_op jit(solution)/shard_map/ppermute | solution.py:293
  36.4 6.7 %copy-start.3 = (bf16[16,16,512]{2,1,0:T(8,128)(2,1)}, bf16[16,16,512]{2,1,0:T(8,128)(2,1)S(1)}, u32[]{:S(2)}) copy-start(bf16[16,16,512]{2,1,0:T(8,128)(2,1)S(1)} %collective-permute-done.1.refs_6_) | copy-start | bytes 786436
  36.4 15.8 %collective-permute-start.9 = (bf16[8,16,512]{2,1,0:T(8,128)(2,1)S(1)}, bf16[8,16,512]{2,1,0:T(8,128)(2,1)S(1)}, u32[]{:S(2)}, u32[]{:S(2)}) collective-permute-start(bf16[8,16,512]{2,1,0:T(8,128)(2,1)S(1)} %constant_dynamic-slice_fusion.1), channel_id=1, source_target_pairs={{0,4},{1,13},{2,6},{3,15},{4,8},{5,1},{6,10},{7,3},{8,12},{9,5},{1... | collective-permute-start | bytes 393224 | tf_op jit(solution)/shard_map/ppermute | solution.py:293
  37.4 15.3 %collective-permute-start.7 = (bf16[16,16,512]{2,1,0:T(8,128)(2,1)S(1)}, bf16[16,16,512]{2,1,0:T(8,128)(2,1)S(1)}, u32[]{:S(2)}, u32[]{:S(2)}) collective-permute-start(bf16[16,16,512]{2,1,0:T(8,128)(2,1)S(1)} %collective-permute-done.1.refs_6_), channel_id=1, source_target_pairs={{0,2},{1,15},{2,4},{3,1},{4,6},{5,3},{6,8},{7,5},{8,10},{9,7},{10,... | collective-permute-start | bytes 786440 | tf_op jit(solution)/shard_map/ppermute | solution.py:293
  38.1 5.0 %copy-start.2 = (bf16[16,16,512]{2,1,0:T(8,128)(2,1)}, bf16[16,16,512]{2,1,0:T(8,128)(2,1)S(1)}, u32[]{:S(2)}) copy-start(bf16[16,16,512]{2,1,0:T(8,128)(2,1)S(1)} %collective-permute-done.5.refs_7_) | copy-start | bytes 786436
  38.1 15.4 %collective-permute-start.2 = (bf16[16,16,512]{2,1,0:T(8,128)(2,1)S(1)}, bf16[16,16,512]{2,1,0:T(8,128)(2,1)S(1)}, u32[]{:S(2)}, u32[]{:S(2)}) collective-permute-start(bf16[16,16,512]{2,1,0:T(8,128)(2,1)S(1)} %collective-permute-done.1.refs_6_), channel_id=1, source_target_pairs={{0,1},{1,0},{2,3},{3,2},{4,5},{5,4},{6,7},{7,6},{8,9},{9,8},{10,11... | collective-permute-start | bytes 786440 | tf_op jit(solution)/shard_map/ppermute | solution.py:293
  40.4 2.7 %copy-start.15 = (bf16[16,16,512]{2,1,0:T(8,128)(2,1)}, bf16[16,16,512]{2,1,0:T(8,128)(2,1)S(1)}, u32[]{:S(2)}) copy-start(bf16[16,16,512]{2,1,0:T(8,128)(2,1)S(1)} %collective-permute-done.11.refs_4_) | copy-start | bytes 786436
  40.4 12.2 %collective-permute-start.10 = (bf16[8,16,512]{2,1,0:T(8,128)(2,1)S(1)}, bf16[8,16,512]{2,1,0:T(8,128)(2,1)S(1)}, u32[]{:S(2)}, u32[]{:S(2)}) collective-permute-start(bf16[8,16,512]{2,1,0:T(8,128)(2,1)S(1)} %constant_dynamic-slice_fusion), channel_id=1, source_target_pairs={{0,4},{1,13},{2,6},{3,15},{4,8},{5,1},{6,10},{7,3},{8,12},{9,5},{1... | collective-permute-start | bytes 393224 | tf_op jit(solution)/shard_map/ppermute | solution.py:293
  41.9 1.3 %copy-start.16 = (bf16[16,16,512]{2,1,0:T(8,128)(2,1)}, bf16[16,16,512]{2,1,0:T(8,128)(2,1)S(1)}, u32[]{:S(2)}) copy-start(bf16[16,16,512]{2,1,0:T(8,128)(2,1)S(1)} %collective-permute-done.12.refs_5_) | copy-start | bytes 786436
  41.9 10.8 %collective-permute-start.8 = (bf16[16,16,512]{2,1,0:T(8,128)(2,1)S(1)}, bf16[16,16,512]{2,1,0:T(8,128)(2,1)S(1)}, u32[]{:S(2)}, u32[]{:S(2)}) collective-permute-start(bf16[16,16,512]{2,1,0:T(8,128)(2,1)S(1)} %collective-permute-done.5.refs_7_), channel_id=1, source_target_pairs={{0,2},{1,15},{2,4},{3,1},{4,6},{5,3},{6,8},{7,5},{8,10},{9,7},{10,... | collective-permute-start | bytes 786440 | tf_op jit(solution)/shard_map/ppermute | solution.py:293
  52.2 2.9 %copy-start.19 = (bf16[8,16,512]{2,1,0:T(8,128)(2,1)}, bf16[8,16,512]{2,1,0:T(8,128)(2,1)S(1)}, u32[]{:S(2)}) copy-start(bf16[8,16,512]{2,1,0:T(8,128)(2,1)S(1)} %collective-permute-done.9.refs_6_) | copy-start | bytes 393220
  52.2 1.9 %collective-permute-start.6 = (bf16[16,16,512]{2,1,0:T(8,128)(2,1)}, bf16[16,16,512]{2,1,0:T(8,128)(2,1)S(1)}, u32[]{:S(2)}, u32[]{:S(2)}) collective-permute-start(bf16[16,16,512]{2,1,0:T(8,128)(2,1)} %copy-done.2), channel_id=1, source_target_pairs={{0,1},{1,0},{2,3},{3,2},{4,5},{5,4},{6,7},{7,6},{8,9},{9,8},{10,11... | collective-permute-start | bytes 786440 | tf_op jit(solution)/shard_map/ppermute | solution.py:293
  52.7 2.4 %copy-start.9 = (bf16[16,16,512]{2,1,0:T(8,128)(2,1)}, bf16[16,16,512]{2,1,0:T(8,128)(2,1)S(1)}, u32[]{:S(2)}) copy-start(bf16[16,16,512]{2,1,0:T(8,128)(2,1)S(1)} %collective-permute-done.7.refs_2_) | copy-start | bytes 786436
  52.7 2.4 %copy-start.20 = (bf16[8,16,512]{2,1,0:T(8,128)(2,1)}, bf16[8,16,512]{2,1,0:T(8,128)(2,1)S(1)}, u32[]{:S(2)}) copy-start(bf16[8,16,512]{2,1,0:T(8,128)(2,1)S(1)} %collective-permute-done.10.refs_8_) | copy-start | bytes 393220
  52.7 2.4 %copy-start.13 = (bf16[16,16,512]{2,1,0:T(8,128)(2,1)}, bf16[16,16,512]{2,1,0:T(8,128)(2,1)S(1)}, u32[]{:S(2)}) copy-start(bf16[16,16,512]{2,1,0:T(8,128)(2,1)S(1)} %collective-permute-done.8.refs_3_) | copy-start | bytes 786436
  52.7 2.4 %collective-permute-start.13 = (bf16[16,16,512]{2,1,0:T(8,128)(2,1)S(1)}, bf16[16,16,512]{2,1,0:T(8,128)(2,1)S(1)}, u32[]{:S(2)}, u32[]{:S(2)}) collective-permute-start(bf16[16,16,512]{2,1,0:T(8,128)(2,1)S(1)} %collective-permute-done.7.refs_2_), channel_id=1, source_target_pairs={{0,1},{1,0},{2,3},{3,2},{4,5},{5,4},{6,7},{7,6},{8,9},{9,8},{10,11... | collective-permute-start | bytes 786440 | tf_op jit(solution)/shard_map/ppermute | solution.py:293
  53.0 2.1 %collective-permute-start.14 = (bf16[16,16,512]{2,1,0:T(8,128)(2,1)S(1)}, bf16[16,16,512]{2,1,0:T(8,128)(2,1)S(1)}, u32[]{:S(2)}, u32[]{:S(2)}) collective-permute-start(bf16[16,16,512]{2,1,0:T(8,128)(2,1)S(1)} %collective-permute-done.8.refs_3_), channel_id=1, source_target_pairs={{0,1},{1,0},{2,3},{3,2},{4,5},{5,4},{6,7},{7,6},{8,9},{9,8},{10,11... | collective-permute-start | bytes 786440 | tf_op jit(solution)/shard_map/ppermute | solution.py:293
  53.3 1.6 %collective-permute-start.16 = (bf16[8,16,512]{2,1,0:T(8,128)(2,1)S(1)}, bf16[8,16,512]{2,1,0:T(8,128)(2,1)S(1)}, u32[]{:S(2)}, u32[]{:S(2)}) collective-permute-start(bf16[8,16,512]{2,1,0:T(8,128)(2,1)S(1)} %collective-permute-done.9.refs_6_), channel_id=1, source_target_pairs={{0,1},{1,0},{2,3},{3,2},{4,5},{5,4},{6,7},{7,6},{8,9},{9,8},{10,11... | collective-permute-start | bytes 393224 | tf_op jit(solution)/shard_map/ppermute | solution.py:293
  53.5 1.6 %copy-start.11 = (bf16[16,16,512]{2,1,0:T(8,128)(2,1)}, bf16[16,16,512]{2,1,0:T(8,128)(2,1)S(1)}, u32[]{:S(2)}) copy-start(bf16[16,16,512]{2,1,0:T(8,128)(2,1)S(1)} %collective-permute-done.2.refs_0_) | copy-start | bytes 786436
  53.5 1.6 %collective-permute-start.15 = (bf16[8,16,512]{2,1,0:T(8,128)(2,1)S(1)}, bf16[8,16,512]{2,1,0:T(8,128)(2,1)S(1)}, u32[]{:S(2)}, u32[]{:S(2)}) collective-permute-start(bf16[8,16,512]{2,1,0:T(8,128)(2,1)S(1)} %collective-permute-done.10.refs_8_), channel_id=1, source_target_pairs={{0,1},{1,0},{2,3},{3,2},{4,5},{5,4},{6,7},{7,6},{8,9},{9,8},{10,11... | collective-permute-start | bytes 393224 | tf_op jit(solution)/shard_map/ppermute | solution.py:293
  54.0 1.1 %copy-start.14 = (bf16[16,16,512]{2,1,0:T(8,128)(2,1)}, bf16[16,16,512]{2,1,0:T(8,128)(2,1)S(1)}, u32[]{:S(2)}) copy-start(bf16[16,16,512]{2,1,0:T(8,128)(2,1)S(1)} %collective-permute-done.6.refs_1_) | copy-start | bytes 786436
  54.9 0.7 copy-start.21
  55.1 0.7 copy-start.22
  55.1 0.7 copy-start.17
  55.1 0.9 %copy-start.18 = (bf16[16,16,512]{2,1,0:T(8,128)(2,1)}, bf16[16,16,512]{2,1,0:T(8,128)(2,1)S(1)}, u32[]{:S(2)}) copy-start(bf16[16,16,512]{2,1,0:T(8,128)(2,1)S(1)} %collective-permute-done.14.refs_5_) | copy-start | bytes 786436
